TPU v7x, 32 devices: a whole 2x2x4 slice. The times are simulated.
32 devices in a mesh: ctx: 8 (over z, y), tp: 4 (over x, core).
Axes of the slice: x: 2, y: 2, z: 4, core: 2. Of those that a mesh axis runs over, the one named last changes fastest.
Arguments:
- query: bfloat16 [4096, 6144], P('ctx', 'tp'), may hold values from -6 to 6
- key_in: bfloat16 [4096, 6144], P('ctx', 'tp'), may hold values from -6 to 6
- value_in: bfloat16 [4096, 6144], P('ctx', 'tp'), may hold values from -6 to 6
- dout: bfloat16 [4096, 6144], P('ctx', 'tp'), may hold values from -0.5 to 0.5
- summary_offset: int32 [1], replicated, may hold values from 0 to 31
Outputs:
- grad_query: bfloat16 [4096, 6144], P(('ctx', 'tp'))
- grad_key: bfloat16 [4096, 6144], P(('ctx', 'tp'))
- grad_value: bfloat16 [4096, 6144], P(('ctx', 'tp'))
Inputs may be any that keep to these rules, and one draw needn't show every extreme that they name: Summary block s is block s * 32 + summary_offset[s].
All inputs are finite; a program needn't handle non-finite values.
Results may differ from a plain program's by a relative error of at most 0.014.
Values may be sent and summed in bfloat16 or wider, within the bound.
A program may use at most 128 MiB of HBM per device.

v0:
```python
import jax
import jax.numpy as jnp
from jax import lax
from jax.sharding import PartitionSpec as P

HDIM = 128
BLOCK = 128
BAND = 8
STRIDE = 32
REACH = 2


def passed_along(value, axis, steps):
    count = lax.axis_size(axis)
    leading, last = (max(0, -steps), min(count, count - steps))
    return lax.ppermute(value, axis, [(source, source + steps) for source in range(leading, last)])


def broadcast(value, axis, source):
    kept = jnp.where(lax.axis_index(axis) == source, value, 0).astype(value.dtype)
    return lax.psum(kept, axis)


def band_mask(query_tok, key_tok):
    return (
        (key_tok >= 0)
        & (key_tok <= query_tok)
        & (key_tok // BLOCK >= query_tok // BLOCK - (BAND - 1))
    )


def column(array, start):
    return lax.dynamic_slice_in_dim(array, start, HDIM, 1)


def in_summary(tokens, groups):
    return jnp.any((tokens // BLOCK)[:, None] == groups[None, :], axis=1)


def on_device(query, key_in, value_in, dout, summary_offset):
    rows, width = query.shape
    heads_here = width // HDIM
    me = lax.axis_index("ctx")
    n_ctx = lax.axis_size("ctx")
    scale = HDIM ** (-0.5)
    n_sum = summary_offset.shape[0]
    groups = jnp.arange(n_sum, dtype=jnp.int32) * STRIDE + summary_offset
    owner = groups * BLOCK // rows
    local_start = groups * BLOCK - owner * rows
    within = jnp.arange(BLOCK, dtype=jnp.int32)
    tile_rows = (local_start[:, None] + within[None, :]).reshape(-1)
    sum_tok = (groups[:, None] * BLOCK + within[None, :]).reshape(-1)
    sum_owner = jnp.repeat(owner, BLOCK)
    mine = (sum_owner == me)[:, None]

    def fetch(distance):
        return passed_along((key_in, value_in), "ctx", distance)

    fetched = [fetch(distance) for distance in range(REACH, 0, -1)]
    ext_k = jnp.concatenate([piece[0] for piece in fetched] + [key_in], axis=0)
    ext_v = jnp.concatenate([piece[1] for piece in fetched] + [value_in], axis=0)

    def fill(index, carry):
        start = local_start[index]
        tile = (
            lax.dynamic_slice_in_dim(key_in, start, BLOCK, 0),
            lax.dynamic_slice_in_dim(value_in, start, BLOCK, 0),
        )
        got_k, got_v = (
            broadcast(tile[0], "ctx", owner[index]),
            broadcast(tile[1], "ctx", owner[index]),
        )
        return (
            lax.dynamic_update_slice_in_dim(carry[0], got_k, index * BLOCK, 0),
            lax.dynamic_update_slice_in_dim(carry[1], got_v, index * BLOCK, 0),
        )

    empty = jnp.zeros((n_sum * BLOCK, width), jnp.bfloat16)
    sum_k, sum_v = lax.fori_loop(0, n_sum, fill, (empty, empty))
    key_all = jnp.concatenate([ext_k, sum_k], axis=0)
    value_all = jnp.concatenate([ext_v, sum_v], axis=0)
    query_tok = me * rows + jnp.arange(rows, dtype=jnp.int32)
    ext_tok = (me - REACH) * rows + jnp.arange((REACH + 1) * rows, dtype=jnp.int32)
    elsewhere = in_summary(ext_tok, groups) & (ext_tok < me * rows)
    band_part = (
        band_mask(query_tok[:, None], ext_tok[None, :]) & jnp.logical_not(elsewhere)[None, :]
    )
    sum_block = (sum_tok // BLOCK)[None, :]
    query_block = (query_tok // BLOCK)[:, None]
    before_band = sum_block < query_block - (BAND - 1)
    inside_band = (
        (sum_block >= query_block - (BAND - 1))
        & (sum_block <= query_block)
        & (sum_owner != me)[None, :]
    )
    summary_ok = before_band | inside_band
    allowed = jnp.concatenate([band_part, summary_ok], axis=1)
    first_key = REACH * rows
    kept = key_all.shape[0] - first_key

    def own_head(head, carry):
        grad_q, grad_k, grad_v, lse_all, delta_all = carry
        start = head * HDIM
        rows_q = column(query, start)
        rows_do = column(dout, start)
        keys = column(key_all, start)
        values = column(value_all, start)
        scores = jnp.einsum("qd,kd->qk", rows_q, keys, preferred_element_type=jnp.float32) * scale
        top = jnp.max(jnp.where(allowed, scores, -jnp.inf), axis=1, keepdims=True)
        total = jnp.sum(jnp.where(allowed, jnp.exp(scores - top), 0.0), axis=1, keepdims=True)
        lse = top + jnp.log(total)
        prob = jnp.where(allowed, jnp.exp(scores - lse), 0.0)
        dprob = jnp.einsum("qd,kd->qk", rows_do, values, preferred_element_type=jnp.float32)
        delta = jnp.sum(prob * dprob, axis=1, keepdims=True)
        dscore = (prob * (dprob - delta)).astype(jnp.bfloat16)
        prob_low = prob.astype(jnp.bfloat16)
        head_q = (
            jnp.einsum("qk,kd->qd", dscore, keys, preferred_element_type=jnp.float32) * scale
        ).astype(jnp.bfloat16)
        head_k = (
            jnp.einsum(
                "qk,qd->kd", dscore[:, first_key:], rows_q, preferred_element_type=jnp.float32
            )
            * scale
        )
        head_v = jnp.einsum(
            "qk,qd->kd", prob_low[:, first_key:], rows_do, preferred_element_type=jnp.float32
        )
        grad_q = lax.dynamic_update_slice_in_dim(grad_q, head_q, start, 1)
        grad_k = lax.dynamic_update_slice_in_dim(grad_k, head_k, start, 1)
        grad_v = lax.dynamic_update_slice_in_dim(grad_v, head_v, start, 1)
        lse_all = lax.dynamic_update_slice_in_dim(lse_all, lse.reshape(1, rows), head, 0)
        delta_all = lax.dynamic_update_slice_in_dim(delta_all, delta.reshape(1, rows), head, 0)
        return (grad_q, grad_k, grad_v, lse_all, delta_all)

    start_carry = (
        jnp.zeros((rows, width), jnp.bfloat16),
        jnp.zeros((kept, width), jnp.float32),
        jnp.zeros((kept, width), jnp.float32),
        jnp.zeros((heads_here, rows), jnp.float32),
        jnp.zeros((heads_here, rows), jnp.float32),
    )
    grad_q, grad_k, grad_v, lse_all, delta_all = lax.fori_loop(0, heads_here, own_head, start_carry)

    def remote_terms(later_q, later_do, later_lse, later_delta, later_mask):

        def remote_head(head, carry):
            acc_k, acc_v = carry
            start = head * HDIM
            rows_q = column(later_q, start)
            rows_do = column(later_do, start)
            keys = column(key_in, start)
            values = column(value_in, start)
            lse = lax.dynamic_slice_in_dim(later_lse, head, 1, 0).reshape(rows, 1)
            delta = lax.dynamic_slice_in_dim(later_delta, head, 1, 0).reshape(rows, 1)
            scores = (
                jnp.einsum("qd,kd->qk", rows_q, keys, preferred_element_type=jnp.float32) * scale
            )
            prob = jnp.where(later_mask, jnp.exp(scores - lse), 0.0)
            dprob = jnp.einsum("qd,kd->qk", rows_do, values, preferred_element_type=jnp.float32)
            dscore = (prob * (dprob - delta)).astype(jnp.bfloat16)
            prob_low = prob.astype(jnp.bfloat16)
            head_k = (
                jnp.einsum("qk,qd->kd", dscore, rows_q, preferred_element_type=jnp.float32) * scale
            )
            head_v = jnp.einsum("qk,qd->kd", prob_low, rows_do, preferred_element_type=jnp.float32)
            acc_k = lax.dynamic_update_slice_in_dim(acc_k, column(acc_k, start) + head_k, start, 1)
            acc_v = lax.dynamic_update_slice_in_dim(acc_v, column(acc_v, start) + head_v, start, 1)
            return (acc_k, acc_v)

        return remote_head

    local_k = grad_k[:rows]
    local_v = grad_v[:rows]
    local_tok = me * rows + jnp.arange(rows, dtype=jnp.int32)
    local_plain = jnp.logical_not(in_summary(local_tok, groups))[None, :]
    for distance in range(1, REACH + 1):
        inputs = passed_along((query, dout), "ctx", -distance)
        stats = passed_along((lse_all, delta_all), "ctx", -distance)
        (later_q, later_do), (later_lse, later_delta) = (inputs, stats)
        later_tok = (me + distance) * rows + jnp.arange(rows, dtype=jnp.int32)
        later_mask = (
            band_mask(later_tok[:, None], local_tok[None, :])
            & (later_tok < n_ctx * rows)[:, None]
            & local_plain
        )
        local_k, local_v = lax.fori_loop(
            0,
            heads_here,
            remote_terms(later_q, later_do, later_lse, later_delta, later_mask),
            (local_k, local_v),
        )
    summary_k = grad_k[rows:]
    summary_v = grad_v[rows:]
    total_k, total_v = lax.psum((summary_k, summary_v), "ctx")
    local_k = local_k.at[tile_rows].add(jnp.where(mine, total_k, 0.0))
    local_v = local_v.at[tile_rows].add(jnp.where(mine, total_v, 0.0))
    moved = (
        lax.all_to_all(grad_q, "tp", split_axis=0, concat_axis=1, tiled=True),
        lax.all_to_all(local_k.astype(jnp.bfloat16), "tp", split_axis=0, concat_axis=1, tiled=True),
        lax.all_to_all(local_v.astype(jnp.bfloat16), "tp", split_axis=0, concat_axis=1, tiled=True),
    )
    return (moved[0], moved[1], moved[2])


def solution(mesh):
    return jax.shard_map(
        on_device,
        mesh=mesh,
        in_specs=(P("ctx", "tp"), P("ctx", "tp"), P("ctx", "tp"), P("ctx", "tp"), P()),
        out_specs=(P(("ctx", "tp"), None), P(("ctx", "tp"), None), P(("ctx", "tp"), None)),
        check_vma=False,
    )
```

profile of v0, /device:TPU:0, one launch (start us, length us, event | category | flops | bytes accessed | tf_op | source)
XLA Modules:
  0.0 575.6 jit_solution(4237955092773513969)
XLA Ops:
  7.2 5.0 collective-permute-start
  12.2 4.6 collective-permute-start.1
  16.8 3.5 collective-permute-start.2
  20.3 4.6 collective-permute-start.3
  32.1 23.7 %collective-permute-done = bf16[512,1536]{1,0:T(8,128)(2,1)S(1)} collective-permute-done((bf16[512,1536]{1,0:T(8,128)(2,1)}, bf16[512,1536]{1,0:T(8,128)(2,1)S(1)}, u32[]{:S(2)}, u32[]{:S(2)}) %collective-permute-start) | collective-permute-done | bytes 1572896 | tf_op jit(solution)/shard_map/ppermute | solution.py:16
  57.0 31.8 %collective-permute-done.1 = bf16[512,1536]{1,0:T(8,128)(2,1)} collective-permute-done((bf16[512,1536]{1,0:T(8,128)(2,1)}, bf16[512,1536]{1,0:T(8,128)(2,1)}, u32[]{:S(2)}, u32[]{:S(2)}) %collective-permute-start.1) | collective-permute-done | bytes 1572896 | tf_op jit(solution)/shard_map/ppermute | solution.py:16
  90.1 82.5 %all-reduce.7.cloned.1.call-done = (bf16[128,1536]{1,0:T(8,128)(2,1)}, bf16[128,1536]{1,0:T(8,128)(2,1)}) async-done(((bf16[128,1536]{1,0:T(8,128)(2,1)}, bf16[128,1536]{1,0:T(8,128)(2,1)}), (bf16[128,1536]{1,0:T(8,128)(2,1)}, bf16[128,1536]{1,0:T(8,128)(2,1)})) %all-reduce.7.cloned.1.call-update) | async-done | bytes 786448 | tf_op jit(solution)/shard_map/while/body/eval_jaxpr/psum | solution.py:21
  172.6 5.8 %pad_maximum_fusion = bf16[1664,1536]{1,0:T(8,128)(2,1)} fusion(bf16[128,1536]{1,0:T(8,128)(2,1)} %get-tuple-element.737, bf16[512,1536]{1,0:T(8,128)(2,1)} %param.12, bf16[512,1536]{1,0:T(8,128)(2,1)} %collective-permute-done.1, bf16[512,1536]{1,0:T(8,128)(2,1)} %copy-done.2), kind=kLoop, calls=%fused_computation.84 | loop fusion | flops 20447232 | bytes 10223616 | tf_op jit(solution)/shard_map/concatenate | solution.py:80
  178.4 4.8 pad_maximum_fusion.1
  189.3 145.8 %while.59 = (s32[]{:T(128)}, bf16[512,1536]{1,0:T(8,128)(2,1)}, f32[640,1536]{1,0:T(8,128)}, f32[640,1536]{1,0:T(8,128)}, f32[12,512]{1,0:T(8,128)S(1)}, /*index...) while((s32[]{:T(128)}, bf16[512,1536]{1,0:T(8,128)(2,1)}, ...), condition=%wide.region_6.7_spmd, body=%wide.region_2.6_spmd.sunk | while | flops 833371136 | bytes 33750208 | solution.py:143
  339.8 3.7 slice.26
  345.6 3.8 slice.27
  349.4 4.4 all-to-all-start
  358.7 75.4 %while.60 = (s32[]{:T(128)}, f32[512,1536]{1,0:T(8,128)}, f32[512,1536]{1,0:T(8,128)}, bf16[512,1536]{1,0:T(8,128)(2,1)}, bf16[512,1536]{1,0:T(8,128)(2,1)}, /*i...) while((s32[]{:T(128)}, f32[512,1536]{1,0:T(8,128)}, ...), condition=%wide.region_8.9_spmd.clone, body=%wide.region_7.8_spmd.clone.sunk | while | flops 272039936 | bytes 5007079 | solution.py:187
  387.5 2.6 fusion.142
  393.8 2.6 fusion.142
  400.1 2.6 fusion.142
  406.3 2.6 fusion.142
  418.9 2.6 fusion.142
  434.1 75.4 %while.61 = (s32[]{:T(128)}, f32[512,1536]{1,0:T(8,128)}, f32[512,1536]{1,0:T(8,128)}, bf16[512,1536]{1,0:T(8,128)(2,1)}, bf16[512,1536]{1,0:T(8,128)(2,1)}, /*i...) while((s32[]{:T(128)}, f32[512,1536]{1,0:T(8,128)}, ...), condition=%wide.region_10.11_spmd.clone, body=%wide.region_9.10_spmd.clone.sunk | while | flops 272039936 | bytes 5007079 | solution.py:187
  450.4 2.6 fusion.152
  462.9 2.6 fusion.152
  469.2 2.6 fusion.152
  475.5 2.6 fusion.152
  481.8 2.6 fusion.152
  509.5 5.4 scatter_custom_fusion.1
  514.8 3.4 convert_element_type.60
  518.2 4.3 all-to-all-start.2
  522.6 3.0 scatter_custom_fusion
  526.9 15.8 %all-to-all-done.2 = bf16[4,128,1536]{2,1,0:T(8,128)(2,1)} async-done(((bf16[4,128,1536]{2,1,0:T(8,128)(2,1)}), bf16[4,128,1536]{2,1,0:T(8,128)(2,1)}, u32[]{:S(2)}, u32[]{:S(2)}) %all-to-all-start.2) | async-done | bytes 1572896 | tf_op jit(solution)/shard_map/all_to_all | solution.py:201
  542.7 3.6 all-to-all-start.1
  553.3 13.1 %all-to-all-done.1 = bf16[4,128,1536]{2,1,0:T(8,128)(2,1)S(1)} async-done(((bf16[4,128,1536]{2,1,0:T(8,128)(2,1)}), bf16[4,128,1536]{2,1,0:T(8,128)(2,1)S(1)}, u32[]{:S(2)}, u32[]{:S(2)}) %all-to-all-start.1) | async-done | bytes 1572896 | tf_op jit(solution)/shard_map/all_to_all | solution.py:200
  (268 shorter events, 307.3 us)
Async XLA Ops:
  7.2 165.4 %all-reduce.7.cloned.1.call-start = ((), (), s32[]{:S(2)}) async-start(), calls=%async_computation.4 | async-start | bytes 1572864 | tf_op jit(solution)/shard_map/while/body/eval_jaxpr/psum | solution.py:21
  7.2 48.5 %collective-permute-start = (bf16[512,1536]{1,0:T(8,128)(2,1)}, bf16[512,1536]{1,0:T(8,128)(2,1)S(1)}, u32[]{:S(2)}, u32[]{:S(2)}) collective-permute-start(bf16[512,1536]{1,0:T(8,128)(2,1)} %param.12), channel_id=1, source_target_pairs={{0,8},{4,12},{8,16},{12,20},{16,24},{20,28},{1,9},{5,13},{9,17},{1... | collective-permute-start | bytes 4718600 | tf_op jit(solution)/shard_map/ppermute | solution.py:16
  12.2 76.6 %collective-permute-start.1 = (bf16[512,1536]{1,0:T(8,128)(2,1)}, bf16[512,1536]{1,0:T(8,128)(2,1)}, u32[]{:S(2)}, u32[]{:S(2)}) collective-permute-start(bf16[512,1536]{1,0:T(8,128)(2,1)} %param.12), channel_id=1, source_target_pairs={{0,4},{4,8},{8,12},{12,16},{16,20},{20,24},{24,28},{1,5},{5,9},{9,... | collective-permute-start | bytes 4718600 | tf_op jit(solution)/shard_map/ppermute | solution.py:16
  16.8 161.6 %collective-permute-start.2 = (bf16[512,1536]{1,0:T(8,128)(2,1)}, bf16[512,1536]{1,0:T(8,128)(2,1)}, u32[]{:S(2)}, u32[]{:S(2)}) collective-permute-start(bf16[512,1536]{1,0:T(8,128)(2,1)} %param.13), channel_id=1, source_target_pairs={{0,8},{4,12},{8,16},{12,20},{16,24},{20,28},{1,9},{5,13},{9,17},{1... | collective-permute-start | bytes 4718600 | tf_op jit(solution)/shard_map/ppermute | solution.py:16
  20.3 158.1 %collective-permute-start.3 = (bf16[512,1536]{1,0:T(8,128)(2,1)}, bf16[512,1536]{1,0:T(8,128)(2,1)}, u32[]{:S(2)}, u32[]{:S(2)}) collective-permute-start(bf16[512,1536]{1,0:T(8,128)(2,1)} %param.13), channel_id=1, source_target_pairs={{0,4},{4,8},{8,12},{12,16},{16,20},{20,24},{24,28},{1,5},{5,9},{9,... | collective-permute-start | bytes 4718600 | tf_op jit(solution)/shard_map/ppermute | solution.py:16
  24.9 331.0 %collective-permute-start.6 = (bf16[512,1536]{1,0:T(8,128)(2,1)}, bf16[512,1536]{1,0:T(8,128)(2,1)}, u32[]{:S(2)}, u32[]{:S(2)}) collective-permute-start(bf16[512,1536]{1,0:T(8,128)(2,1)} %param.14), channel_id=1, source_target_pairs={{4,0},{8,4},{12,8},{16,12},{20,16},{24,20},{28,24},{5,1},{9,5},{13... | collective-permute-start | bytes 4718600 | tf_op jit(solution)/shard_map/ppermute | solution.py:16
  55.8 116.8 %copy-start.2 = (bf16[512,1536]{1,0:T(8,128)(2,1)}, bf16[512,1536]{1,0:T(8,128)(2,1)S(1)}, u32[]{:S(2)}) copy-start(bf16[512,1536]{1,0:T(8,128)(2,1)S(1)} %collective-permute-done) | copy-start | bytes 4718596
  55.8 378.3 %collective-permute-start.10 = (bf16[512,1536]{1,0:T(8,128)(2,1)}, bf16[512,1536]{1,0:T(8,128)(2,1)}, u32[]{:S(2)}, u32[]{:S(2)}) collective-permute-start(bf16[512,1536]{1,0:T(8,128)(2,1)} %param.14), channel_id=1, source_target_pairs={{8,0},{12,4},{16,8},{20,12},{24,16},{28,20},{9,1},{13,5},{17,9},{2... | collective-permute-start | bytes 4718600 | tf_op jit(solution)/shard_map/ppermute | solution.py:16
  88.8 265.7 %collective-permute-start.4 = (bf16[512,1536]{1,0:T(8,128)(2,1)}, bf16[512,1536]{1,0:T(8,128)(2,1)}, u32[]{:S(2)}, u32[]{:S(2)}) collective-permute-start(bf16[512,1536]{1,0:T(8,128)(2,1)} %param.11), channel_id=1, source_target_pairs={{4,0},{8,4},{12,8},{16,12},{20,16},{24,20},{28,24},{5,1},{9,5},{13... | collective-permute-start | bytes 4718600 | tf_op jit(solution)/shard_map/ppermute | solution.py:16
  172.6 5.8 %copy-start.1 = (bf16[512,1536]{1,0:T(8,128)(2,1)S(1)}, bf16[512,1536]{1,0:T(8,128)(2,1)}, u32[]{:S(2)}) copy-start(bf16[512,1536]{1,0:T(8,128)(2,1)} %param.13) | copy-start | bytes 4718596
  172.6 5.8 %copy-start.3 = (bf16[128,1536]{1,0:T(8,128)(2,1)S(1)}, bf16[128,1536]{1,0:T(8,128)(2,1)}, u32[]{:S(2)}) copy-start(bf16[128,1536]{1,0:T(8,128)(2,1)} %get-tuple-element.738) | copy-start | bytes 1179652
  335.2 22.0 %collective-permute-start.5 = (f32[12,512]{1,0:T(8,128)S(1)}, f32[12,512]{1,0:T(8,128)S(1)}, u32[]{:S(2)}, u32[]{:S(2)}) collective-permute-start(f32[12,512]{1,0:T(8,128)S(1)} %get-tuple-element.558), channel_id=1, source_target_pairs={{4,0},{8,4},{12,8},{16,12},{20,16},{24,20},{28,24},{5,1},{9,5},{13... | collective-permute-start | bytes 73736 | tf_op jit(solution)/shard_map/ppermute | solution.py:16
  336.5 22.2 %collective-permute-start.7 = (f32[12,512]{1,0:T(8,128)S(1)}, f32[12,512]{1,0:T(8,128)S(1)}, u32[]{:S(2)}, u32[]{:S(2)}) collective-permute-start(f32[12,512]{1,0:T(8,128)S(1)} %get-tuple-element.559), channel_id=1, source_target_pairs={{4,0},{8,4},{12,8},{16,12},{20,16},{24,20},{28,24},{5,1},{9,5},{13... | collective-permute-start | bytes 73736 | tf_op jit(solution)/shard_map/ppermute | solution.py:16
  349.4 168.8 %all-to-all-start = ((bf16[4,128,1536]{2,1,0:T(8,128)(2,1)}), bf16[4,128,1536]{2,1,0:T(8,128)(2,1)}, u32[]{:S(2)}, u32[]{:S(2)}) async-start(bf16[4,128,1536]{2,1,0:T(8,128)(2,1)} %bitcast.41), calls=%async_computation | async-start | bytes 3145728 | tf_op jit(solution)/shard_map/all_to_all | solution.py:199
  353.8 155.7 %all-reduce.5.cloned.1.call-start = ((), (), s32[]{:S(2)}) async-start(), calls=%async_computation.3 | async-start | bytes 3145728 | tf_op jit(solution)/shard_map/psum | solution.py:195
  354.6 79.5 %collective-permute-start.8 = (bf16[512,1536]{1,0:T(8,128)(2,1)}, bf16[512,1536]{1,0:T(8,128)(2,1)}, u32[]{:S(2)}, u32[]{:S(2)}) collective-permute-start(bf16[512,1536]{1,0:T(8,128)(2,1)} %get-tuple-element.1241), channel_id=1, source_target_pairs={{8,0},{12,4},{16,8},{20,12},{24,16},{28,20},{9,1},{13,5},{17,9},{2... | collective-permute-start | bytes 4718600 | tf_op jit(solution)/shard_map/ppermute | solution.py:16
  355.9 78.2 %collective-permute-start.11 = (f32[12,512]{1,0:T(8,128)S(1)}, f32[12,512]{1,0:T(8,128)S(1)}, u32[]{:S(2)}, u32[]{:S(2)}) collective-permute-start(f32[12,512]{1,0:T(8,128)S(1)} %get-tuple-element.559), channel_id=1, source_target_pairs={{8,0},{12,4},{16,8},{20,12},{24,16},{28,20},{9,1},{13,5},{17,9},{2... | collective-permute-start | bytes 73736 | tf_op jit(solution)/shard_map/ppermute | solution.py:16
  357.2 76.9 %collective-permute-start.9 = (f32[12,512]{1,0:T(8,128)S(1)}, f32[12,512]{1,0:T(8,128)S(1)}, u32[]{:S(2)}, u32[]{:S(2)}) collective-permute-start(f32[12,512]{1,0:T(8,128)S(1)} %get-tuple-element.558), channel_id=1, source_target_pairs={{8,0},{12,4},{16,8},{20,12},{24,16},{28,20},{9,1},{13,5},{17,9},{2... | collective-permute-start | bytes 73736 | tf_op jit(solution)/shard_map/ppermute | solution.py:16
  514.8 7.7 %copy-start = (f32[512,1536]{1,0:T(8,128)S(1)}, f32[512,1536]{1,0:T(8,128)}, u32[]{:S(2)}) copy-start(f32[512,1536]{1,0:T(8,128)} %get-tuple-element.562) | copy-start | bytes 9437188
  518.2 24.5 %all-to-all-start.2 = ((bf16[4,128,1536]{2,1,0:T(8,128)(2,1)}), bf16[4,128,1536]{2,1,0:T(8,128)(2,1)}, u32[]{:S(2)}, u32[]{:S(2)}) async-start(bf16[4,128,1536]{2,1,0:T(8,128)(2,1)} %bitcast.45), calls=%async_computation.2 | async-start | bytes 3145728 | tf_op jit(solution)/shard_map/all_to_all | solution.py:201
  542.7 23.6 %all-to-all-start.1 = ((bf16[4,128,1536]{2,1,0:T(8,128)(2,1)}), bf16[4,128,1536]{2,1,0:T(8,128)(2,1)S(1)}, u32[]{:S(2)}, u32[]{:S(2)}) async-start(bf16[4,128,1536]{2,1,0:T(8,128)(2,1)} %bitcast.46), calls=%async_computation.1 | async-start | bytes 3145728 | tf_op jit(solution)/shard_map/all_to_all | solution.py:200
Sparse Core Ops, SparseCore 0:
  30.6 141.9 all-reduce.6
  359.2 110.2 all-reduce.4
where the time goes:
time: 584 us; the launch traced here: 576 us
  matrix products  279 us (48%)
  waiting for transfers between devices  168 us (29%)
  other arithmetic  44.5 us (8%)
  starting transfers between devices  40.5 us (7%)
  local copies, waits for them, and re-layouts  28.5 us (5%)
  between operations  15.1 us (3%)
    psum x1, waiting for transfers between devices, broadcast(): return lax.psum(kept, axis)  82.5 us
    dot_general x24, matrix products, remote_head(): jnp.einsum('qk,qd->kd', dscore, rows_q, preferred_element_type=jnp.float32)  61.5 us
    ppermute x12, waiting for transfers between devices, passed_along(): lax.ppermute(value, axis, [(source, source + steps) for source in range(l...  55.5 us
    dot_general x24, matrix products, remote_head(): jnp.einsum('qk,qd->kd', prob_low, rows_do, preferred_element_type=jnp.flo...  50.9 us
    dot_general x24, matrix products, remote_head(): jnp.einsum('qd,kd->qk', rows_q, keys, preferred_element_type=jnp.float32)  37.8 us
    ppermute x12, starting transfers between devices, passed_along(): lax.ppermute(value, axis, [(source, source + steps) for source in range(l...  28.1 us
    dot_general x12, matrix products, own_head(): jnp.einsum('qd,kd->qk', rows_do, values, preferred_element_type=jnp.float32)  28 us
    dot_general x12, matrix products, own_head(): jnp.einsum('qk,kd->qd', dscore, keys, preferred_element_type=jnp.float32)  27.4 us
  transfers between devices with their start and end apart: 17, of which 5 were waited for; matrix products, arithmetic and copies ran while one was open for 61% of the time, Pallas kernels for 0%

commit v1 on v0

v1 whole, which is shorter than its diff:
```python
import functools
import math

import jax
import jax.numpy as jnp
from jax import lax
from jax.experimental import pallas as pl
from jax.experimental.pallas import tpu as pltpu
from jax.sharding import PartitionSpec as P

HDIM = 128
BLOCK = 128
BAND = 8
STRIDE = 32
REACH = 2
PAIR = 2 * BLOCK
CHUNKS = 3


def shifted(value, axis, steps):
    count = lax.axis_size(axis)
    leading, last = (max(0, -steps), min(count, count - steps))
    return lax.ppermute(value, axis, [(source, source + steps) for source in range(leading, last)])


def swapped(value, axis):
    count = lax.axis_size(axis)
    return lax.ppermute(value, axis, [(source, source ^ 1) for source in range(count)])


def attend(n_sum, info, q, do, kv2, kv1, kv0, kvs, gq, p2, p1, p0, ps):
    me = info[0]
    rows = q.shape[0]
    blocks = rows // BLOCK
    band = (BAND + 1) * BLOCK
    scale = HDIM ** (-0.5)
    key_at = lax.broadcasted_iota(jnp.int32, (band, PAIR), 0)
    query_at = lax.broadcasted_iota(jnp.int32, (1, PAIR), 1)
    last = query_at + (BAND - 1) * BLOCK
    second = query_at // BLOCK
    parts = []
    for pair in range(rows // PAIR):
        low = REACH * blocks + 2 * pair - (BAND - 1)
        pieces = []
        for index, ref in enumerate((kv2, kv1, kv0)):
            start = max(low - index * blocks, 0) * BLOCK
            stop = min(low + BAND + 1 - index * blocks, blocks) * BLOCK
            pieces.append((ref, start, stop))
        keys = jnp.concatenate([r[0, a:b] for r, a, b in pieces] + [kvs[0]], axis=0)
        values = jnp.concatenate([r[1, a:b] for r, a, b in pieces] + [kvs[1]], axis=0)
        span = slice(pair * PAIR, (pair + 1) * PAIR)
        rows_q = q[span]
        rows_do = do[span]
        scores = lax.dot_general(
            keys, rows_q, (((1,), (1,)), ((), ())), preferred_element_type=jnp.float32
        )
        first = jnp.maximum(second, (REACH - me) * blocks - low) * BLOCK
        ok = (key_at >= first) & (key_at <= last)
        masked = [jnp.where(ok, scores[:band], -jnp.inf)]
        query_block = me * blocks + 2 * pair + second
        for s in range(n_sum):
            ok_s = info[1 + s] < query_block - (BAND - 1)
            tile = scores[band + s * BLOCK : band + (s + 1) * BLOCK]
            masked.append(jnp.where(ok_s, tile, -jnp.inf))
        scores = jnp.concatenate(masked, axis=0)
        top = jnp.max(scores, axis=0, keepdims=True)
        raw = jnp.exp2((scores - top) * (scale * math.log2(math.e)))
        inverse = 1.0 / jnp.sum(raw, axis=0, keepdims=True)
        prob = raw * inverse
        dprob = lax.dot_general(
            values, rows_do, (((1,), (1,)), ((), ())), preferred_element_type=jnp.float32
        )
        delta = jnp.sum(prob * dprob, axis=0, keepdims=True)
        dscore = (prob * (dprob - delta)).astype(jnp.bfloat16)
        prob_low = prob.astype(jnp.bfloat16)
        part_v = jnp.dot(prob_low, rows_do, preferred_element_type=jnp.float32)
        part_k = jnp.dot(dscore, rows_q, preferred_element_type=jnp.float32) * scale
        grad_q = lax.dot_general(
            keys, dscore, (((0,), (0,)), ((), ())), preferred_element_type=jnp.float32
        )
        gq[span] = (grad_q * scale).T.astype(gq.dtype)
        parts.append((low, part_k, part_v))
    for index, out in enumerate((p2, p1, p0)):
        for which in range(2):
            for block in range(blocks):
                total = None
                for part in parts:
                    at = index * blocks + block - part[0]
                    if 0 <= at <= BAND:
                        piece = part[1 + which][at * BLOCK : (at + 1) * BLOCK]
                        total = piece if total is None else total + piece
                if total is None:
                    total = jnp.zeros((BLOCK, HDIM), jnp.float32)
                out[which, block * BLOCK : (block + 1) * BLOCK] = total.astype(out.dtype)
    for which in range(2):
        total = parts[0][1 + which][band:]
        for part in parts[1:]:
            total = total + part[1 + which][band:]
        ps[which] = total


def attention(info, query, dout, kv2, kv1, kv0, kvs, first_head, n_sum):
    rows = query.shape[0]
    width = kv0.shape[2]
    heads = width // HDIM
    mine = pl.BlockSpec((rows, HDIM), lambda h: (0, first_head + h))
    wide = pl.BlockSpec((2, rows, HDIM), lambda h: (0, 0, h))
    tile = pl.BlockSpec((2, n_sum * BLOCK, HDIM), lambda h: (0, 0, h))
    pairs = rows // PAIR * (BAND + 1 + n_sum) * BLOCK * PAIR
    return pl.pallas_call(
        functools.partial(attend, n_sum),
        grid=(heads,),
        in_specs=[pl.BlockSpec(memory_space=pltpu.SMEM), mine, mine, wide, wide, wide, tile],
        out_specs=[
            pl.BlockSpec((rows, HDIM), lambda h: (0, h)),
            wide,
            wide,
            wide,
            tile,
        ],
        out_shape=[
            jax.ShapeDtypeStruct((rows, width), jnp.bfloat16),
            jax.ShapeDtypeStruct((2, rows, width), jnp.bfloat16),
            jax.ShapeDtypeStruct((2, rows, width), jnp.bfloat16),
            jax.ShapeDtypeStruct((2, rows, width), jnp.float32),
            jax.ShapeDtypeStruct((2, n_sum * BLOCK, width), jnp.float32),
        ],
        compiler_params=pltpu.CompilerParams(vmem_limit_bytes=40 * 1024 * 1024),
        cost_estimate=pl.CostEstimate(
            flops=heads * pairs * 10 * HDIM,
            bytes_accessed=heads * rows * HDIM * 32,
            transcendentals=heads * pairs,
        ),
    )(info, query, dout, kv2, kv1, kv0, kvs)


def on_device(query, key_in, value_in, dout, summary_offset):
    rows, width = query.shape
    me = lax.axis_index("ctx")
    n_ctx = lax.axis_size("ctx")
    n_tp = lax.axis_size("tp")
    n_sum = summary_offset.shape[0]
    groups = jnp.arange(n_sum, dtype=jnp.int32) * STRIDE + summary_offset
    owner = groups * BLOCK // rows
    local_start = groups * BLOCK - owner * rows
    distance = me - owner
    tile_distance = jnp.repeat(distance, BLOCK)[None, :, None]
    info = jnp.concatenate([me.astype(jnp.int32)[None], groups])
    odd = me % 2 == 1
    jumps = []
    reached = REACH + 1
    while reached < n_ctx:
        jumps.append(reached)
        reached *= 2
    part = width // CHUNKS
    heads = part // HDIM

    ready = []
    for chunk in range(CHUNKS):
        span = slice(chunk * part, (chunk + 1) * part)
        kv0 = jnp.stack([key_in[:, span], value_in[:, span]])
        kv2 = shifted(kv0, "ctx", 2)
        kv1 = swapped(jnp.where(odd, kv2, kv0), "ctx")
        tiles = []
        for s in range(n_sum):
            at = (0, local_start[s], 0)
            size = (2, BLOCK, part)
            far = lax.dynamic_slice(kv2, at, size)
            near = lax.dynamic_slice(kv1, at, size)
            own = lax.dynamic_slice(kv0, at, size)
            tiles.append(
                jnp.where(distance[s] == 2, far, jnp.where(distance[s] == 1, near, own))
            )
        kvs = jnp.concatenate(tiles, axis=1)
        for jump in jumps:
            got = shifted(kvs, "ctx", jump)
            kvs = jnp.where((tile_distance >= jump) & (tile_distance < 2 * jump), got, kvs)
        ready.append((kv2, kv1, kv0, kvs))

    grads = []
    for chunk in range(CHUNKS):
        gq, p2, p1, p0, ps = attention(
            info, query, dout, *ready[chunk], chunk * heads, n_sum
        )
        moved_q = lax.all_to_all(gq, "tp", split_axis=0, concat_axis=1, tiled=True)
        for jump in reversed(jumps):
            got = shifted(ps.astype(jnp.bfloat16), "ctx", -jump).astype(jnp.float32)
            ps = jnp.where((tile_distance >= 0) & (tile_distance < jump), ps + got, ps)

        def add_tile(array, s, away):
            at = (0, local_start[s], 0)
            piece = lax.dynamic_slice(array, at, (2, BLOCK, part)).astype(jnp.float32)
            term = jnp.where(distance[s] == away, ps[:, s * BLOCK : (s + 1) * BLOCK], 0.0)
            return lax.dynamic_update_slice(array, (piece + term).astype(array.dtype), at)

        for s in range(n_sum):
            p2 = add_tile(p2, s, 2)
            p1 = add_tile(p1, s, 1)
            p0 = add_tile(p0, s, 0)
        near = swapped(p1, "ctx").astype(jnp.float32)
        p2 = jnp.where(odd, p2.astype(jnp.float32) + near, p2.astype(jnp.float32))
        far = shifted(p2.astype(jnp.bfloat16), "ctx", -2).astype(jnp.float32)
        total = (p0 + jnp.where(odd, 0.0, near) + far).astype(jnp.bfloat16)
        moved_kv = lax.all_to_all(total, "tp", split_axis=1, concat_axis=2, tiled=True)
        grads.append((moved_q, moved_kv[0], moved_kv[1]))

    def joined(pieces):
        split = [piece.reshape(rows // n_tp, n_tp, part) for piece in pieces]
        return jnp.concatenate(split, axis=2).reshape(rows // n_tp, n_tp * width)

    return tuple(joined([grad[which] for grad in grads]) for which in range(3))


def solution(mesh):
    return jax.shard_map(
        on_device,
        mesh=mesh,
        in_specs=(P("ctx", "tp"), P("ctx", "tp"), P("ctx", "tp"), P("ctx", "tp"), P()),
        out_specs=(P(("ctx", "tp"), None), P(("ctx", "tp"), None), P(("ctx", "tp"), None)),
        check_vma=False,
    )
```

time: 584 us -> 356 us (0.61); the launches traced: 576 us -> 354 us
  matrix products: 279 us -> 0 us
  starting transfers between devices: 40.5 us -> 118 us
  waiting for transfers between devices: 168 us -> 117 us
  Pallas kernels: 0 us -> 48 us
  between operations: 15.1 us -> 2.09 us
    dot_general x132 -> x0, matrix products: 279 us -> none  [the longest x24 61.5 us: remote_head(): jnp.einsum('qk,qd->kd', dscore, rows_q, preferred_element_type=jnp.float32)]
    psum x2 -> x0, waiting for transfers between devices: 82.5 us -> none  [the longest x1 82.5 us: broadcast(): return lax.psum(kept, axis)]
    ppermute x12 -> x24, starting transfers between devices: 28.1 us -> 93 us  [the longest x18 81.5 us: shifted(): lax.ppermute(value, axis, [(source, source + steps) for source in range(l...]
    pallas_call x0 -> x3, Pallas kernels: none -> 48 us  [attention(): pl.pallas_call(functools.partial(attend, n_sum), grid=(heads,), in_specs=...]
    ppermute x12 -> x24, waiting for transfers between devices: 55.5 us -> 102 us  [the longest x18 89.3 us: shifted(): lax.ppermute(value, axis, [(source, source + steps) for source in range(l...]
    all_to_all x3 -> x6, waiting for transfers between devices: 28.9 us -> 15.3 us  [the longest x3 9.62 us: on_device(): lax.all_to_all(total, 'tp', split_axis=1, concat_axis=2, tiled=True)]
    all_to_all x3 -> x6, starting transfers between devices: 12.3 us -> 24.7 us  [the longest x3 12.4 us: on_device(): moved_q = lax.all_to_all(gq, 'tp', split_axis=0, concat_axis=1, tiled=True)]
    dynamic_update_slice x0 -> x9, other arithmetic: none -> 11.9 us  [add_tile(): lax.dynamic_update_slice(array, (piece + term).astype(array.dtype), at)]
  transfers between devices with their start and end apart: 17 -> 30, of which waited for: 5 -> 14; matrix products, arithmetic and copies ran while one was open for 61% -> 15% of each run, Pallas kernels for 0% -> 14%
where the time goes in v1:
time: 356 us; the launch traced here: 354 us
  starting transfers between devices  118 us (33%)
  waiting for transfers between devices  117 us (33%)
  Pallas kernels  48 us (13%)
  other arithmetic  43.9 us (12%)
  local copies, waits for them, and re-layouts  25.5 us (7%)
    ppermute x18, waiting for transfers between devices, shifted(): lax.ppermute(value, axis, [(source, source + steps) for source in range(l...  89.3 us
    ppermute x18, starting transfers between devices, shifted(): lax.ppermute(value, axis, [(source, source + steps) for source in range(l...  81.5 us
    pallas_call x3, Pallas kernels, attention(): pl.pallas_call(functools.partial(attend, n_sum), grid=(heads,), in_specs=...  48 us
    all_to_all x3, starting transfers between devices, on_device(): moved_q = lax.all_to_all(gq, 'tp', split_axis=0, concat_axis=1, tiled=True)  12.4 us
    all_to_all x3, starting transfers between devices, on_device(): lax.all_to_all(total, 'tp', split_axis=1, concat_axis=2, tiled=True)  12.3 us
    ppermute x6, waiting for transfers between devices, swapped(): lax.ppermute(value, axis, [(source, source ^ 1) for source in range(count)])  12.3 us
    dynamic_update_slice x9, other arithmetic, add_tile(): lax.dynamic_update_slice(array, (piece + term).astype(array.dtype), at)  11.9 us
    ppermute x6, starting transfers between devices, swapped(): lax.ppermute(value, axis, [(source, source ^ 1) for source in range(count)])  11.5 us
  transfers between devices with their start and end apart: 30, of which 14 were waited for; matrix products, arithmetic and copies ran while one was open for 15% of the time, Pallas kernels for 14%

profile of v1, /device:TPU:0, one launch (start us, length us, event | category | flops | bytes accessed | tf_op | source)
XLA Modules:
  0.0 354.0 jit_solution(7061013470579055048)
XLA Ops:
  4.0 5.0 %collective-permute-start = (bf16[2,512,512]{2,1,0:T(8,128)(2,1)}, bf16[2,512,512]{2,1,0:T(8,128)(2,1)S(1)}, u32[]{:S(2)}, u32[]{:S(2)}) collective-permute-start(bf16[2,512,512]{2,1,0:T(8,128)(2,1)} %pad_maximum_fusion.2.kv0), channel_id=1, source_target_pairs={{0,8},{4,12},{8,16},{12,20},{16,24},{20,28},{1,9},{5,13},{9,17},{1... | collective-permute-start | bytes 3145736 | tf_op jit(solution)/shard_map/ppermute | solution.py:23
  10.0 3.5 collective-permute-start.4
  14.6 3.5 collective-permute-start.8
  18.1 14.6 %collective-permute-done.kv2 = bf16[2,512,512]{2,1,0:T(8,128)(2,1)S(1)} collective-permute-done((bf16[2,512,512]{2,1,0:T(8,128)(2,1)}, bf16[2,512,512]{2,1,0:T(8,128)(2,1)S(1)}, u32[]{:S(2)}, u32[]{:S(2)}) %collective-permute-start) | collective-permute-done | bytes 1048608 | tf_op jit(solution)/shard_map/ppermute | solution.py:23
  36.7 18.6 %collective-permute-done.4.kv2 = bf16[2,512,512]{2,1,0:T(8,128)(2,1)S(1)} collective-permute-done((bf16[2,512,512]{2,1,0:T(8,128)(2,1)}, bf16[2,512,512]{2,1,0:T(8,128)(2,1)S(1)}, u32[]{:S(2)}, u32[]{:S(2)}) %collective-permute-start.4) | collective-permute-done | bytes 1048608 | tf_op jit(solution)/shard_map/ppermute | solution.py:23
  58.1 18.5 %collective-permute-done.8.kv2 = bf16[2,512,512]{2,1,0:T(8,128)(2,1)S(1)} collective-permute-done((bf16[2,512,512]{2,1,0:T(8,128)(2,1)}, bf16[2,512,512]{2,1,0:T(8,128)(2,1)S(1)}, u32[]{:S(2)}, u32[]{:S(2)}) %collective-permute-start.8) | collective-permute-done | bytes 1048608 | tf_op jit(solution)/shard_map/ppermute | solution.py:23
  81.3 4.2 %collective-permute-start.2 = (bf16[2,128,512]{2,1,0:T(8,128)(2,1)S(1)}, bf16[2,128,512]{2,1,0:T(8,128)(2,1)S(1)}, u32[]{:S(2)}, u32[]{:S(2)}) collective-permute-start(bf16[2,128,512]{2,1,0:T(8,128)(2,1)S(1)} %fusion.29), channel_id=1, source_target_pairs={{0,12},{4,16},{8,20},{12,24},{16,28},{1,13},{5,17},{9,21},{13,25},... | collective-permute-start | bytes 786440 | tf_op jit(solution)/shard_map/ppermute | solution.py:23
  86.8 5.7 %collective-permute-start.6 = (bf16[2,128,512]{2,1,0:T(8,128)(2,1)S(1)}, bf16[2,128,512]{2,1,0:T(8,128)(2,1)S(1)}, u32[]{:S(2)}, u32[]{:S(2)}) collective-permute-start(bf16[2,128,512]{2,1,0:T(8,128)(2,1)S(1)} %fusion.26), channel_id=1, source_target_pairs={{0,12},{4,16},{8,20},{12,24},{16,28},{1,13},{5,17},{9,21},{13,25},... | collective-permute-start | bytes 786440 | tf_op jit(solution)/shard_map/ppermute | solution.py:23
  92.6 10.7 %collective-permute-done.9.kv1 = bf16[2,512,512]{2,1,0:T(8,128)(2,1)} collective-permute-done((bf16[2,512,512]{2,1,0:T(8,128)(2,1)}, bf16[2,512,512]{2,1,0:T(8,128)(2,1)}, u32[]{:S(2)}, u32[]{:S(2)}) %collective-permute-start.9) | collective-permute-done | bytes 1048608 | tf_op jit(solution)/shard_map/ppermute | solution.py:28
  104.4 16.5 %collective-permute-start.10 = (bf16[2,128,512]{2,1,0:T(8,128)(2,1)S(1)}, bf16[2,128,512]{2,1,0:T(8,128)(2,1)S(1)}, u32[]{:S(2)}, u32[]{:S(2)}) collective-permute-start(bf16[2,128,512]{2,1,0:T(8,128)(2,1)S(1)} %fusion.23), channel_id=1, source_target_pairs={{0,12},{4,16},{8,20},{12,24},{16,28},{1,13},{5,17},{9,21},{13,25},... | collective-permute-start | bytes 786440 | tf_op jit(solution)/shard_map/ppermute | solution.py:23
  124.6 2.9 collective-permute-done.10
  127.6 27.7 %collective-permute-start.11 = (bf16[2,128,512]{2,1,0:T(8,128)(2,1)S(1)}, bf16[2,128,512]{2,1,0:T(8,128)(2,1)S(1)}, u32[]{:S(2)}, u32[]{:S(2)}) collective-permute-start(bf16[2,128,512]{2,1,0:T(8,128)(2,1)S(1)} %broadcast_select_fusion.3), channel_id=1, source_target_pairs={{0,24},{4,28},{1,25},{5,29},{2,26},{6,30},{3,27},{7,31}} | collective-permute-start | bytes 786440 | tf_op jit(solution)/shard_map/ppermute | solution.py:23
  155.4 16.1 %shard_map.76 = (bf16[512,512]{1,0:T(8,128)(2,1)S(1)}, bf16[2,512,512]{2,1,0:T(8,128)(2,1)S(1)}, bf16[2,512,512]{2,1,0:T(8,128)(2,1)}, f32[2,512,512]{2,1,0:T(8,128)S(1)}, f32[2,128,512]{2,1,0:T(8,128)S(1)}) custom-call(s32[2]{0:T(128)S(1)} %pad_add_fusion.info, bf16[512,1536]{1,0:T(8,128)(2,1)S(1)} %copy-done.16, bf16[512,1536]{1,0:T(8,128)(2,1)S(1)} %copy-done.17, ...), custom_call_target="tpu_custom_call" | custom-call | flops 3355443200 | bytes 8388608 | tf_op jit(solution)/shard_map/pallas_call | solution.py:110
  174.2 16.0 %shard_map.77 = (bf16[512,512]{1,0:T(8,128)(2,1)S(1)}, bf16[2,512,512]{2,1,0:T(8,128)(2,1)S(1)}, bf16[2,512,512]{2,1,0:T(8,128)(2,1)}, f32[2,512,512]{2,1,0:T(8,128)S(1)}, f32[2,128,512]{2,1,0:T(8,128)S(1)}) custom-call(s32[2]{0:T(128)S(1)} %pad_add_fusion.info, bf16[512,1536]{1,0:T(8,128)(2,1)S(1)} %copy-done.16, bf16[512,1536]{1,0:T(8,128)(2,1)S(1)} %copy-done.17, ...), custom_call_target="tpu_custom_call" | custom-call | flops 3355443200 | bytes 8388608 | tf_op jit(solution)/shard_map/pallas_call | solution.py:110
  193.0 10.3 %collective-permute-done.16 = bf16[2,128,512]{2,1,0:T(8,128)(2,1)S(1)} collective-permute-done((bf16[2,128,512]{2,1,0:T(8,128)(2,1)S(1)}, bf16[2,128,512]{2,1,0:T(8,128)(2,1)S(1)}, u32[]{:S(2)}, u32[]{:S(2)}) %collective-permute-start.16) | collective-permute-done | bytes 262176 | tf_op jit(solution)/shard_map/ppermute | solution.py:23
  207.7 16.0 %shard_map.78 = (bf16[512,512]{1,0:T(8,128)(2,1)S(1)}, bf16[2,512,512]{2,1,0:T(8,128)(2,1)S(1)}, bf16[2,512,512]{2,1,0:T(8,128)(2,1)}, f32[2,512,512]{2,1,0:T(8,128)S(1)}, f32[2,128,512]{2,1,0:T(8,128)S(1)}) custom-call(s32[2]{0:T(128)S(1)} %pad_add_fusion.info, bf16[512,1536]{1,0:T(8,128)(2,1)S(1)} %copy-done.16, bf16[512,1536]{1,0:T(8,128)(2,1)S(1)} %copy-done.17, ...), custom_call_target="tpu_custom_call" | custom-call | flops 3355443200 | bytes 8388608 | tf_op jit(solution)/shard_map/pallas_call | solution.py:110
  228.1 4.2 %all-to-all-start = ((bf16[4,128,512]{2,1,0:T(8,128)(2,1)}), bf16[4,128,512]{2,1,0:T(8,128)(2,1)}, u32[]{:S(2)}, u32[]{:S(2)}) async-start(bf16[4,128,512]{2,1,0:T(8,128)(2,1)} %bitcast.54), calls=%async_computation | async-start | bytes 1048576 | tf_op jit(solution)/shard_map/all_to_all | solution.py:185
  241.1 2.5 fusion.9
  244.9 8.8 %collective-permute-done.21 = bf16[2,128,512]{2,1,0:T(8,128)(2,1)S(1)} collective-permute-done((bf16[2,128,512]{2,1,0:T(8,128)(2,1)S(1)}, bf16[2,128,512]{2,1,0:T(8,128)(2,1)S(1)}, u32[]{:S(2)}, u32[]{:S(2)}) %collective-permute-start.21) | collective-permute-done | bytes 262176 | tf_op jit(solution)/shard_map/ppermute | solution.py:23
  258.1 4.9 %collective-permute-start.22 = (bf16[2,512,512]{2,1,0:T(8,128)(2,1)}, bf16[2,512,512]{2,1,0:T(8,128)(2,1)}, u32[]{:S(2)}, u32[]{:S(2)}) collective-permute-start(bf16[2,512,512]{2,1,0:T(8,128)(2,1)} %fusion.19), channel_id=1, source_target_pairs={{0,4},{4,0},{8,12},{12,8},{16,20},{20,16},{24,28},{28,24},{1,5},{5... | collective-permute-start | bytes 3145736 | tf_op jit(solution)/shard_map/ppermute | solution.py:28
  263.1 4.1 %all-to-all-start.1 = ((bf16[4,128,512]{2,1,0:T(8,128)(2,1)}), bf16[4,128,512]{2,1,0:T(8,128)(2,1)}, u32[]{:S(2)}, u32[]{:S(2)}) async-start(bf16[4,128,512]{2,1,0:T(8,128)(2,1)} %bitcast.53), calls=%async_computation.1 | async-start | bytes 1048576 | tf_op jit(solution)/shard_map/all_to_all | solution.py:185
  272.5 3.6 %all-to-all-done.1 = bf16[4,128,512]{2,1,0:T(8,128)(2,1)} async-done(((bf16[4,128,512]{2,1,0:T(8,128)(2,1)}), bf16[4,128,512]{2,1,0:T(8,128)(2,1)}, u32[]{:S(2)}, u32[]{:S(2)}) %all-to-all-start.1) | async-done | bytes 524320 | tf_op jit(solution)/shard_map/all_to_all | solution.py:185
  276.1 4.1 %all-to-all-start.2 = ((bf16[4,128,512]{2,1,0:T(8,128)(2,1)}), bf16[4,128,512]{2,1,0:T(8,128)(2,1)}, u32[]{:S(2)}, u32[]{:S(2)}) async-start(bf16[4,128,512]{2,1,0:T(8,128)(2,1)} %bitcast.55), calls=%async_computation.2 | async-start | bytes 1048576 | tf_op jit(solution)/shard_map/all_to_all | solution.py:185
  282.4 2.6 fusion.2
  289.2 4.3 %all-to-all-start.3 = ((bf16[2,512,512]{2,0,1:T(2,128)(2,1)}), bf16[2,512,512]{2,0,1:T(2,128)(2,1)}, u32[]{:S(2)}, u32[]{:S(2)}) async-start(bf16[2,512,512]{2,0,1:T(2,128)(2,1)} %copy.36), calls=%async_computation.3 | async-start | bytes 2097152 | tf_op jit(solution)/shard_map/all_to_all | solution.py:204
  293.5 2.6 fusion.11
  297.5 3.8 %collective-permute-done.19 = bf16[2,512,512]{2,1,0:T(8,128)(2,1)} collective-permute-done((bf16[2,512,512]{2,1,0:T(8,128)(2,1)}, bf16[2,512,512]{2,1,0:T(8,128)(2,1)}, u32[]{:S(2)}, u32[]{:S(2)}) %collective-permute-start.19) | collective-permute-done | bytes 1048608 | tf_op jit(solution)/shard_map/ppermute | solution.py:23
  305.4 2.6 all-to-all-done.3
  308.0 4.5 %all-to-all-start.4 = ((bf16[2,512,512]{2,0,1:T(2,128)(2,1)}), bf16[2,512,512]{2,0,1:T(2,128)(2,1)}, u32[]{:S(2)}, u32[]{:S(2)}) async-start(bf16[2,512,512]{2,0,1:T(2,128)(2,1)} %copy.38), calls=%async_computation.4 | async-start | bytes 2097152 | tf_op jit(solution)/shard_map/all_to_all | solution.py:204
  312.6 11.8 %collective-permute-done.23 = bf16[2,512,512]{2,1,0:T(8,128)(2,1)} collective-permute-done((bf16[2,512,512]{2,1,0:T(8,128)(2,1)}, bf16[2,512,512]{2,1,0:T(8,128)(2,1)}, u32[]{:S(2)}, u32[]{:S(2)}) %collective-permute-start.23) | collective-permute-done | bytes 1048608 | tf_op jit(solution)/shard_map/ppermute | solution.py:23
  328.5 3.5 all-to-all-start.5
  339.4 7.0 %all-to-all-done.5 = bf16[2,512,512]{2,0,1:T(2,128)(2,1)S(1)} async-done(((bf16[2,512,512]{2,0,1:T(2,128)(2,1)}), bf16[2,512,512]{2,0,1:T(2,128)(2,1)S(1)}, u32[]{:S(2)}, u32[]{:S(2)}) %all-to-all-start.5) | async-done | bytes 1048608 | tf_op jit(solution)/shard_map/all_to_all | solution.py:204
  (158 shorter events, 87.3 us)
Async XLA Ops:
  4.0 28.8 %collective-permute-start = (bf16[2,512,512]{2,1,0:T(8,128)(2,1)}, bf16[2,512,512]{2,1,0:T(8,128)(2,1)S(1)}, u32[]{:S(2)}, u32[]{:S(2)}) collective-permute-start(bf16[2,512,512]{2,1,0:T(8,128)(2,1)} %pad_maximum_fusion.2.kv0), channel_id=1, source_target_pairs={{0,8},{4,12},{8,16},{12,20},{16,24},{20,28},{1,9},{5,13},{9,17},{1... | collective-permute-start | bytes 3145736 | tf_op jit(solution)/shard_map/ppermute | solution.py:23
  10.0 45.2 %collective-permute-start.4 = (bf16[2,512,512]{2,1,0:T(8,128)(2,1)}, bf16[2,512,512]{2,1,0:T(8,128)(2,1)S(1)}, u32[]{:S(2)}, u32[]{:S(2)}) collective-permute-start(bf16[2,512,512]{2,1,0:T(8,128)(2,1)} %pad_maximum_fusion.3.kv0), channel_id=1, source_target_pairs={{0,8},{4,12},{8,16},{12,20},{16,24},{20,28},{1,9},{5,13},{9,17},{1... | collective-permute-start | bytes 3145736 | tf_op jit(solution)/shard_map/ppermute | solution.py:23
  14.6 61.9 %collective-permute-start.8 = (bf16[2,512,512]{2,1,0:T(8,128)(2,1)}, bf16[2,512,512]{2,1,0:T(8,128)(2,1)S(1)}, u32[]{:S(2)}, u32[]{:S(2)}) collective-permute-start(bf16[2,512,512]{2,1,0:T(8,128)(2,1)} %pad_maximum_fusion.4.kv0), channel_id=1, source_target_pairs={{0,8},{4,12},{8,16},{12,20},{16,24},{20,28},{1,9},{5,13},{9,17},{1... | collective-permute-start | bytes 3145736 | tf_op jit(solution)/shard_map/ppermute | solution.py:23
  35.1 44.9 %collective-permute-start.1 = (bf16[2,512,512]{2,1,0:T(8,128)(2,1)}, bf16[2,512,512]{2,1,0:T(8,128)(2,1)}, u32[]{:S(2)}, u32[]{:S(2)}) collective-permute-start(bf16[2,512,512]{2,1,0:T(8,128)(2,1)} %broadcast_select_fusion.2), channel_id=1, source_target_pairs={{0,4},{4,0},{8,12},{12,8},{16,20},{20,16},{24,28},{28,24},{1,5},{5... | collective-permute-start | bytes 3145736 | tf_op jit(solution)/shard_map/ppermute | solution.py:28
  56.5 29.1 %collective-permute-start.5 = (bf16[2,512,512]{2,1,0:T(8,128)(2,1)}, bf16[2,512,512]{2,1,0:T(8,128)(2,1)}, u32[]{:S(2)}, u32[]{:S(2)}) collective-permute-start(bf16[2,512,512]{2,1,0:T(8,128)(2,1)} %broadcast_select_fusion.1), channel_id=1, source_target_pairs={{0,4},{4,0},{8,12},{12,8},{16,20},{20,16},{24,28},{28,24},{1,5},{5... | collective-permute-start | bytes 3145736 | tf_op jit(solution)/shard_map/ppermute | solution.py:28
  77.8 25.5 %collective-permute-start.9 = (bf16[2,512,512]{2,1,0:T(8,128)(2,1)}, bf16[2,512,512]{2,1,0:T(8,128)(2,1)}, u32[]{:S(2)}, u32[]{:S(2)}) collective-permute-start(bf16[2,512,512]{2,1,0:T(8,128)(2,1)} %broadcast_select_fusion), channel_id=1, source_target_pairs={{0,4},{4,0},{8,12},{12,8},{16,20},{20,16},{24,28},{28,24},{1,5},{5... | collective-permute-start | bytes 3145736 | tf_op jit(solution)/shard_map/ppermute | solution.py:28
  81.3 39.5 %collective-permute-start.2 = (bf16[2,128,512]{2,1,0:T(8,128)(2,1)S(1)}, bf16[2,128,512]{2,1,0:T(8,128)(2,1)S(1)}, u32[]{:S(2)}, u32[]{:S(2)}) collective-permute-start(bf16[2,128,512]{2,1,0:T(8,128)(2,1)S(1)} %fusion.29), channel_id=1, source_target_pairs={{0,12},{4,16},{8,20},{12,24},{16,28},{1,13},{5,17},{9,21},{13,25},... | collective-permute-start | bytes 786440 | tf_op jit(solution)/shard_map/ppermute | solution.py:23
  86.8 68.6 %copy-start.16 = (bf16[512,1536]{1,0:T(8,128)(2,1)S(1)}, bf16[512,1536]{1,0:T(8,128)(2,1)}, u32[]{:S(2)}) copy-start(bf16[512,1536]{1,0:T(8,128)(2,1)} %q.5) | copy-start | bytes 4718596
  86.8 68.6 %copy-start.17 = (bf16[512,1536]{1,0:T(8,128)(2,1)S(1)}, bf16[512,1536]{1,0:T(8,128)(2,1)}, u32[]{:S(2)}) copy-start(bf16[512,1536]{1,0:T(8,128)(2,1)} %do.5) | copy-start | bytes 4718596
  86.8 36.4 %collective-permute-start.6 = (bf16[2,128,512]{2,1,0:T(8,128)(2,1)S(1)}, bf16[2,128,512]{2,1,0:T(8,128)(2,1)S(1)}, u32[]{:S(2)}, u32[]{:S(2)}) collective-permute-start(bf16[2,128,512]{2,1,0:T(8,128)(2,1)S(1)} %fusion.26), channel_id=1, source_target_pairs={{0,12},{4,16},{8,20},{12,24},{16,28},{1,13},{5,17},{9,21},{13,25},... | collective-permute-start | bytes 786440 | tf_op jit(solution)/shard_map/ppermute | solution.py:23
  104.4 23.2 %collective-permute-start.10 = (bf16[2,128,512]{2,1,0:T(8,128)(2,1)S(1)}, bf16[2,128,512]{2,1,0:T(8,128)(2,1)S(1)}, u32[]{:S(2)}, u32[]{:S(2)}) collective-permute-start(bf16[2,128,512]{2,1,0:T(8,128)(2,1)S(1)} %fusion.23), channel_id=1, source_target_pairs={{0,12},{4,16},{8,20},{12,24},{16,28},{1,13},{5,17},{9,21},{13,25},... | collective-permute-start | bytes 786440 | tf_op jit(solution)/shard_map/ppermute | solution.py:23
  120.9 34.4 %collective-permute-start.3 = (bf16[2,128,512]{2,1,0:T(8,128)(2,1)S(1)}, bf16[2,128,512]{2,1,0:T(8,128)(2,1)S(1)}, u32[]{:S(2)}, u32[]{:S(2)}) collective-permute-start(bf16[2,128,512]{2,1,0:T(8,128)(2,1)S(1)} %broadcast_select_fusion.5), channel_id=1, source_target_pairs={{0,24},{4,28},{1,25},{5,29},{2,26},{6,30},{3,27},{7,31}} | collective-permute-start | bytes 786440 | tf_op jit(solution)/shard_map/ppermute | solution.py:23
  123.3 50.8 %collective-permute-start.7 = (bf16[2,128,512]{2,1,0:T(8,128)(2,1)S(1)}, bf16[2,128,512]{2,1,0:T(8,128)(2,1)S(1)}, u32[]{:S(2)}, u32[]{:S(2)}) collective-permute-start(bf16[2,128,512]{2,1,0:T(8,128)(2,1)S(1)} %broadcast_select_fusion.4), channel_id=1, source_target_pairs={{0,24},{4,28},{1,25},{5,29},{2,26},{6,30},{3,27},{7,31}} | collective-permute-start | bytes 786440 | tf_op jit(solution)/shard_map/ppermute | solution.py:23
  127.6 65.3 %collective-permute-start.11 = (bf16[2,128,512]{2,1,0:T(8,128)(2,1)S(1)}, bf16[2,128,512]{2,1,0:T(8,128)(2,1)S(1)}, u32[]{:S(2)}, u32[]{:S(2)}) collective-permute-start(bf16[2,128,512]{2,1,0:T(8,128)(2,1)S(1)} %broadcast_select_fusion.3), channel_id=1, source_target_pairs={{0,24},{4,28},{1,25},{5,29},{2,26},{6,30},{3,27},{7,31}} | collective-permute-start | bytes 786440 | tf_op jit(solution)/shard_map/ppermute | solution.py:23
  172.9 18.7 %collective-permute-start.12 = (bf16[2,128,512]{2,1,0:T(8,128)(2,1)S(1)}, bf16[2,128,512]{2,1,0:T(8,128)(2,1)S(1)}, u32[]{:S(2)}, u32[]{:S(2)}) collective-permute-start(bf16[2,128,512]{2,1,0:T(8,128)(2,1)S(1)} %convert_element_type.120), channel_id=1, source_target_pairs={{24,0},{28,4},{25,1},{29,5},{26,2},{30,6},{27,3},{31,7}} | collective-permute-start | bytes 786440 | tf_op jit(solution)/shard_map/ppermute | solution.py:23
  190.3 13.0 %collective-permute-start.16 = (bf16[2,128,512]{2,1,0:T(8,128)(2,1)S(1)}, bf16[2,128,512]{2,1,0:T(8,128)(2,1)S(1)}, u32[]{:S(2)}, u32[]{:S(2)}) collective-permute-start(bf16[2,128,512]{2,1,0:T(8,128)(2,1)S(1)} %convert_element_type.133), channel_id=1, source_target_pairs={{24,0},{28,4},{25,1},{29,5},{26,2},{30,6},{27,3},{31,7}} | collective-permute-start | bytes 786440 | tf_op jit(solution)/shard_map/ppermute | solution.py:23
  191.7 13.9 %collective-permute-start.13 = (bf16[2,128,512]{2,1,0:T(8,128)(2,1)S(1)}, bf16[2,128,512]{2,1,0:T(8,128)(2,1)S(1)}, u32[]{:S(2)}, u32[]{:S(2)}) collective-permute-start(bf16[2,128,512]{2,1,0:T(8,128)(2,1)S(1)} %fusion.12), channel_id=1, source_target_pairs={{12,0},{16,4},{20,8},{24,12},{28,16},{13,1},{17,5},{21,9},{25,13},... | collective-permute-start | bytes 786440 | tf_op jit(solution)/shard_map/ppermute | solution.py:23
  204.1 28.2 %collective-permute-start.17 = (bf16[2,128,512]{2,1,0:T(8,128)(2,1)}, bf16[2,128,512]{2,1,0:T(8,128)(2,1)}, u32[]{:S(2)}, u32[]{:S(2)}) collective-permute-start(bf16[2,128,512]{2,1,0:T(8,128)(2,1)} %fusion.13), channel_id=1, source_target_pairs={{12,0},{16,4},{20,8},{24,12},{28,16},{13,1},{17,5},{21,9},{25,13},... | collective-permute-start | bytes 786440 | tf_op jit(solution)/shard_map/ppermute | solution.py:23
  207.7 33.4 %collective-permute-start.14 = (bf16[2,512,512]{2,1,0:T(8,128)(2,1)}, bf16[2,512,512]{2,1,0:T(8,128)(2,1)}, u32[]{:S(2)}, u32[]{:S(2)}) collective-permute-start(bf16[2,512,512]{2,1,0:T(8,128)(2,1)} %fusion.15), channel_id=1, source_target_pairs={{0,4},{4,0},{8,12},{12,8},{16,20},{20,16},{24,28},{28,24},{1,5},{5... | collective-permute-start | bytes 3145736 | tf_op jit(solution)/shard_map/ppermute | solution.py:28
  226.8 12.0 %collective-permute-start.20 = (bf16[2,128,512]{2,1,0:T(8,128)(2,1)}, bf16[2,128,512]{2,1,0:T(8,128)(2,1)}, u32[]{:S(2)}, u32[]{:S(2)}) collective-permute-start(bf16[2,128,512]{2,1,0:T(8,128)(2,1)} %convert_element_type.146), channel_id=1, source_target_pairs={{24,0},{28,4},{25,1},{29,5},{26,2},{30,6},{27,3},{31,7}} | collective-permute-start | bytes 786440 | tf_op jit(solution)/shard_map/ppermute | solution.py:23
  228.1 35.0 %all-to-all-start = ((bf16[4,128,512]{2,1,0:T(8,128)(2,1)}), bf16[4,128,512]{2,1,0:T(8,128)(2,1)}, u32[]{:S(2)}, u32[]{:S(2)}) async-start(bf16[4,128,512]{2,1,0:T(8,128)(2,1)} %bitcast.54), calls=%async_computation | async-start | bytes 1048576 | tf_op jit(solution)/shard_map/all_to_all | solution.py:185
  236.8 32.0 %collective-permute-start.18 = (bf16[2,512,512]{2,1,0:T(8,128)(2,1)}, bf16[2,512,512]{2,1,0:T(8,128)(2,1)}, u32[]{:S(2)}, u32[]{:S(2)}) collective-permute-start(bf16[2,512,512]{2,1,0:T(8,128)(2,1)} %fusion.17), channel_id=1, source_target_pairs={{0,4},{4,0},{8,12},{12,8},{16,20},{20,16},{24,28},{28,24},{1,5},{5... | collective-permute-start | bytes 3145736 | tf_op jit(solution)/shard_map/ppermute | solution.py:28
  239.8 13.9 %collective-permute-start.21 = (bf16[2,128,512]{2,1,0:T(8,128)(2,1)S(1)}, bf16[2,128,512]{2,1,0:T(8,128)(2,1)S(1)}, u32[]{:S(2)}, u32[]{:S(2)}) collective-permute-start(bf16[2,128,512]{2,1,0:T(8,128)(2,1)S(1)} %fusion.14), channel_id=1, source_target_pairs={{12,0},{16,4},{20,8},{24,12},{28,16},{13,1},{17,5},{21,9},{25,13},... | collective-permute-start | bytes 786440 | tf_op jit(solution)/shard_map/ppermute | solution.py:23
  243.6 38.7 %collective-permute-start.15 = (bf16[2,512,512]{2,1,0:T(8,128)(2,1)}, bf16[2,512,512]{2,1,0:T(8,128)(2,1)}, u32[]{:S(2)}, u32[]{:S(2)}) collective-permute-start(bf16[2,512,512]{2,1,0:T(8,128)(2,1)} %fusion.9), channel_id=1, source_target_pairs={{8,0},{12,4},{16,8},{20,12},{24,16},{28,20},{9,1},{13,5},{17,9},{2... | collective-permute-start | bytes 3145736 | tf_op jit(solution)/shard_map/ppermute | solution.py:23
  258.1 35.3 %collective-permute-start.22 = (bf16[2,512,512]{2,1,0:T(8,128)(2,1)}, bf16[2,512,512]{2,1,0:T(8,128)(2,1)}, u32[]{:S(2)}, u32[]{:S(2)}) collective-permute-start(bf16[2,512,512]{2,1,0:T(8,128)(2,1)} %fusion.19), channel_id=1, source_target_pairs={{0,4},{4,0},{8,12},{12,8},{16,20},{20,16},{24,28},{28,24},{1,5},{5... | collective-permute-start | bytes 3145736 | tf_op jit(solution)/shard_map/ppermute | solution.py:28
  263.1 13.1 %all-to-all-start.1 = ((bf16[4,128,512]{2,1,0:T(8,128)(2,1)}), bf16[4,128,512]{2,1,0:T(8,128)(2,1)}, u32[]{:S(2)}, u32[]{:S(2)}) async-start(bf16[4,128,512]{2,1,0:T(8,128)(2,1)} %bitcast.53), calls=%async_computation.1 | async-start | bytes 1048576 | tf_op jit(solution)/shard_map/all_to_all | solution.py:185
  271.2 30.0 %collective-permute-start.19 = (bf16[2,512,512]{2,1,0:T(8,128)(2,1)}, bf16[2,512,512]{2,1,0:T(8,128)(2,1)}, u32[]{:S(2)}, u32[]{:S(2)}) collective-permute-start(bf16[2,512,512]{2,1,0:T(8,128)(2,1)} %fusion.10), channel_id=1, source_target_pairs={{8,0},{12,4},{16,8},{20,12},{24,16},{28,20},{9,1},{13,5},{17,9},{2... | collective-permute-start | bytes 3145736 | tf_op jit(solution)/shard_map/ppermute | solution.py:23
  276.1 13.0 %all-to-all-start.2 = ((bf16[4,128,512]{2,1,0:T(8,128)(2,1)}), bf16[4,128,512]{2,1,0:T(8,128)(2,1)}, u32[]{:S(2)}, u32[]{:S(2)}) async-start(bf16[4,128,512]{2,1,0:T(8,128)(2,1)} %bitcast.55), calls=%async_computation.2 | async-start | bytes 1048576 | tf_op jit(solution)/shard_map/all_to_all | solution.py:185
  289.2 18.8 %all-to-all-start.3 = ((bf16[2,512,512]{2,0,1:T(2,128)(2,1)}), bf16[2,512,512]{2,0,1:T(2,128)(2,1)}, u32[]{:S(2)}, u32[]{:S(2)}) async-start(bf16[2,512,512]{2,0,1:T(2,128)(2,1)} %copy.36), calls=%async_computation.3 | async-start | bytes 2097152 | tf_op jit(solution)/shard_map/all_to_all | solution.py:204
  296.0 28.4 %collective-permute-start.23 = (bf16[2,512,512]{2,1,0:T(8,128)(2,1)}, bf16[2,512,512]{2,1,0:T(8,128)(2,1)}, u32[]{:S(2)}, u32[]{:S(2)}) collective-permute-start(bf16[2,512,512]{2,1,0:T(8,128)(2,1)} %fusion.11), channel_id=1, source_target_pairs={{8,0},{12,4},{16,8},{20,12},{24,16},{28,20},{9,1},{13,5},{17,9},{2... | collective-permute-start | bytes 3145736 | tf_op jit(solution)/shard_map/ppermute | solution.py:23
  308.0 20.5 %all-to-all-start.4 = ((bf16[2,512,512]{2,0,1:T(2,128)(2,1)}), bf16[2,512,512]{2,0,1:T(2,128)(2,1)}, u32[]{:S(2)}, u32[]{:S(2)}) async-start(bf16[2,512,512]{2,0,1:T(2,128)(2,1)} %copy.38), calls=%async_computation.4 | async-start | bytes 2097152 | tf_op jit(solution)/shard_map/all_to_all | solution.py:204
  328.5 18.0 %all-to-all-start.5 = ((bf16[2,512,512]{2,0,1:T(2,128)(2,1)}), bf16[2,512,512]{2,0,1:T(2,128)(2,1)S(1)}, u32[]{:S(2)}, u32[]{:S(2)}) async-start(bf16[2,512,512]{2,0,1:T(2,128)(2,1)} %copy.40), calls=%async_computation.5 | async-start | bytes 2097152 | tf_op jit(solution)/shard_map/all_to_all | solution.py:204
  (34 other events, 478.8 us)

commit v2 on v1

--- a/solution.py
+++ b/solution.py
@@ -28,8 +28,9 @@
     return lax.ppermute(value, axis, [(source, source ^ 1) for source in range(count)])
 
 
-def attend(n_sum, info, q, do, kv2, kv1, kv0, kvs, gq, p2, p1, p0, ps):
+def attend(n_sum, info, q, do, kv2, kv1, kv0, kvs, after, gq, p2, p1, p0, ps, token):
     me = info[0]
+    token[0] = me
     rows = q.shape[0]
     blocks = rows // BLOCK
     band = (BAND + 1) * BLOCK
@@ -99,7 +100,7 @@
         ps[which] = total
 
 
-def attention(info, query, dout, kv2, kv1, kv0, kvs, first_head, n_sum):
+def attention(info, query, dout, kv2, kv1, kv0, kvs, after, first_head, n_sum):
     rows = query.shape[0]
     width = kv0.shape[2]
     heads = width // HDIM
@@ -110,13 +111,23 @@
     return pl.pallas_call(
         functools.partial(attend, n_sum),
         grid=(heads,),
-        in_specs=[pl.BlockSpec(memory_space=pltpu.SMEM), mine, mine, wide, wide, wide, tile],
+        in_specs=[
+            pl.BlockSpec(memory_space=pltpu.SMEM),
+            mine,
+            mine,
+            wide,
+            wide,
+            wide,
+            tile,
+            pl.BlockSpec(memory_space=pl.ANY),
+        ],
         out_specs=[
             pl.BlockSpec((rows, HDIM), lambda h: (0, h)),
             wide,
             wide,
             wide,
             tile,
+            pl.BlockSpec(memory_space=pltpu.SMEM),
         ],
         out_shape=[
             jax.ShapeDtypeStruct((rows, width), jnp.bfloat16),
@@ -124,6 +135,7 @@
             jax.ShapeDtypeStruct((2, rows, width), jnp.bfloat16),
             jax.ShapeDtypeStruct((2, rows, width), jnp.float32),
             jax.ShapeDtypeStruct((2, n_sum * BLOCK, width), jnp.float32),
+            jax.ShapeDtypeStruct((1,), jnp.int32),
         ],
         compiler_params=pltpu.CompilerParams(vmem_limit_bytes=40 * 1024 * 1024),
         cost_estimate=pl.CostEstimate(
@@ -131,7 +143,7 @@
             bytes_accessed=heads * rows * HDIM * 32,
             transcendentals=heads * pairs,
         ),
-    )(info, query, dout, kv2, kv1, kv0, kvs)
+    )(info, query, dout, kv2, kv1, kv0, kvs, after)
 
 
 def on_device(query, key_in, value_in, dout, summary_offset):
@@ -155,12 +167,14 @@
     part = width // CHUNKS
     heads = part // HDIM
 
-    ready = []
+    stacked = []
     for chunk in range(CHUNKS):
         span = slice(chunk * part, (chunk + 1) * part)
         kv0 = jnp.stack([key_in[:, span], value_in[:, span]])
-        kv2 = shifted(kv0, "ctx", 2)
-        kv1 = swapped(jnp.where(odd, kv2, kv0), "ctx")
+        stacked.append((kv0, shifted(kv0, "ctx", 2)))
+
+    def gathered(kv0, kv2, here):
+        kv1 = swapped(jnp.where(here % 2 == 1, kv2, kv0), "ctx")
         tiles = []
         for s in range(n_sum):
             at = (0, local_start[s], 0)
@@ -175,14 +189,9 @@
         for jump in jumps:
             got = shifted(kvs, "ctx", jump)
             kvs = jnp.where((tile_distance >= jump) & (tile_distance < 2 * jump), got, kvs)
-        ready.append((kv2, kv1, kv0, kvs))
-
-    grads = []
-    for chunk in range(CHUNKS):
-        gq, p2, p1, p0, ps = attention(
-            info, query, dout, *ready[chunk], chunk * heads, n_sum
-        )
-        moved_q = lax.all_to_all(gq, "tp", split_axis=0, concat_axis=1, tiled=True)
+        return kv2, kv1, kv0, kvs
+
+    def returned(p2, p1, p0, ps):
         for jump in reversed(jumps):
             got = shifted(ps.astype(jnp.bfloat16), "ctx", -jump).astype(jnp.float32)
             ps = jnp.where((tile_distance >= 0) & (tile_distance < jump), ps + got, ps)
@@ -197,11 +206,27 @@
             p2 = add_tile(p2, s, 2)
             p1 = add_tile(p1, s, 1)
             p0 = add_tile(p0, s, 0)
-        near = swapped(p1, "ctx").astype(jnp.float32)
-        p2 = jnp.where(odd, p2.astype(jnp.float32) + near, p2.astype(jnp.float32))
+        near = swapped(p1, "ctx")
+        wide = near.astype(jnp.float32)
+        p2 = jnp.where(odd, p2.astype(jnp.float32) + wide, p2.astype(jnp.float32))
         far = shifted(p2.astype(jnp.bfloat16), "ctx", -2).astype(jnp.float32)
-        total = (p0 + jnp.where(odd, 0.0, near) + far).astype(jnp.bfloat16)
-        moved_kv = lax.all_to_all(total, "tp", split_axis=1, concat_axis=2, tiled=True)
+        total = (p0 + jnp.where(odd, 0.0, wide) + far).astype(jnp.bfloat16)
+        return near, lax.all_to_all(total, "tp", split_axis=1, concat_axis=2, tiled=True)
+
+    grads = []
+    tokens = []
+    returns = []
+    for chunk in range(CHUNKS):
+        here = tokens[chunk - 2][0] if chunk >= 2 else me
+        after = returns[chunk - 2] if chunk >= 2 else summary_offset
+        ready = gathered(*stacked[chunk], here)
+        gq, p2, p1, p0, ps, token = attention(
+            info, query, dout, *ready, after, chunk * heads, n_sum
+        )
+        tokens.append(token)
+        moved_q = lax.all_to_all(gq, "tp", split_axis=0, concat_axis=1, tiled=True)
+        near, moved_kv = returned(p2, p1, p0, ps)
+        returns.append(near)
         grads.append((moved_q, moved_kv[0], moved_kv[1]))
 
     def joined(pieces):

time: 356 us -> 333 us (0.935)
  starting transfers between devices: 118 us -> 101 us
  waiting for transfers between devices: 117 us -> 107 us
  local copies, waits for them, and re-layouts: 25.5 us -> 31.6 us
  other arithmetic: 43.9 us -> 39.7 us
    ppermute x18, starting transfers between devices: 81.5 us -> 63.7 us  [shifted(): lax.ppermute(value, axis, [(source, source + steps) for source in range(l...]
    ppermute x18, waiting for transfers between devices: 89.3 us -> 80.7 us  [shifted(): lax.ppermute(value, axis, [(source, source + steps) for source in range(l...]
    unnamed x74 -> x84, local copies, waits for them, and re-layouts: 8.5 us -> 13.6 us
    dynamic_update_slice x9, other arithmetic: 11.9 us -> 8.27 us  [add_tile(): lax.dynamic_update_slice(array, (piece + term).astype(array.dtype), at)]
  transfers between devices with their start and end apart: 30 -> 30, of which waited for: 14 -> 17; matrix products, arithmetic and copies ran while one was open for 15% -> 15% of each run, Pallas kernels for 14% -> 14%
where the time goes in v2:
time: 333 us; the launch traced here: 331 us
  waiting for transfers between devices  107 us (32%)
  starting transfers between devices  101 us (30%)
  Pallas kernels  47.9 us (14%)
  other arithmetic  39.7 us (12%)
  local copies, waits for them, and re-layouts  31.6 us (9%)
  between operations  3.96 us (1%)
    ppermute x18, waiting for transfers between devices, shifted(): lax.ppermute(value, axis, [(source, source + steps) for source in range(l...  80.7 us
    ppermute x18, starting transfers between devices, shifted(): lax.ppermute(value, axis, [(source, source + steps) for source in range(l...  63.7 us
    pallas_call x3, Pallas kernels, attention(): pl.pallas_call(functools.partial(attend, n_sum), grid=(heads,), in_specs=...  47.9 us
    unnamed x84, local copies, waits for them, and re-layouts  13.6 us
    ppermute x6, starting transfers between devices, swapped(): lax.ppermute(value, axis, [(source, source ^ 1) for source in range(count)])  13.3 us
    all_to_all x3, starting transfers between devices, returned(): lax.all_to_all(total, 'tp', split_axis=1, concat_axis=2, tiled=True)  12.2 us
    all_to_all x3, starting transfers between devices, on_device(): moved_q = lax.all_to_all(gq, 'tp', split_axis=0, concat_axis=1, tiled=True)  11.8 us
    all_to_all x3, waiting for transfers between devices, returned(): lax.all_to_all(total, 'tp', split_axis=1, concat_axis=2, tiled=True)  9.32 us
  transfers between devices with their start and end apart: 30, of which 17 were waited for; matrix products, arithmetic and copies ran while one was open for 15% of the time, Pallas kernels for 14%

profile of v2, /device:TPU:0, one launch (start us, length us, event | category | flops | bytes accessed | tf_op | source)
XLA Modules:
  0.0 331.4 jit_solution(15685733147091689425)
XLA Ops:
  0.6 3.1 slice_bitcast_fusion.8
  4.9 5.0 %collective-permute-start = (bf16[2,512,512]{2,1,0:T(8,128)(2,1)}, bf16[2,512,512]{2,1,0:T(8,128)(2,1)S(1)}, u32[]{:S(2)}, u32[]{:S(2)}) collective-permute-start(bf16[2,512,512]{2,1,0:T(8,128)(2,1)} %pad_maximum_fusion.2.kv0), channel_id=1, source_target_pairs={{0,8},{4,12},{8,16},{12,20},{16,24},{20,28},{1,9},{5,13},{9,17},{1... | collective-permute-start | bytes 3145736 | tf_op jit(solution)/shard_map/ppermute | solution.py:23
  10.1 3.5 %collective-permute-start.4 = (bf16[2,512,512]{2,1,0:T(8,128)(2,1)S(1)}, bf16[2,512,512]{2,1,0:T(8,128)(2,1)S(1)}, u32[]{:S(2)}, u32[]{:S(2)}) collective-permute-start(bf16[2,512,512]{2,1,0:T(8,128)(2,1)S(1)} %pad_maximum_fusion.3.kv0), channel_id=1, source_target_pairs={{0,8},{4,12},{8,16},{12,20},{16,24},{20,28},{1,9},{5,13},{9,17},{1... | collective-permute-start | bytes 3145736 | tf_op jit(solution)/shard_map/ppermute | solution.py:23
  13.6 20.1 %collective-permute-done.kv2 = bf16[2,512,512]{2,1,0:T(8,128)(2,1)S(1)} collective-permute-done((bf16[2,512,512]{2,1,0:T(8,128)(2,1)}, bf16[2,512,512]{2,1,0:T(8,128)(2,1)S(1)}, u32[]{:S(2)}, u32[]{:S(2)}) %collective-permute-start) | collective-permute-done | bytes 1048608 | tf_op jit(solution)/shard_map/ppermute | solution.py:23
  37.9 17.0 %collective-permute-done.4.kv2 = bf16[2,512,512]{2,1,0:T(8,128)(2,1)S(1)} collective-permute-done((bf16[2,512,512]{2,1,0:T(8,128)(2,1)S(1)}, bf16[2,512,512]{2,1,0:T(8,128)(2,1)S(1)}, u32[]{:S(2)}, u32[]{:S(2)}) %collective-permute-start.4) | collective-permute-done | bytes 1048608 | tf_op jit(solution)/shard_map/ppermute | solution.py:23
  62.4 5.0 %collective-permute-start.2 = (bf16[2,128,512]{2,1,0:T(8,128)(2,1)S(1)}, bf16[2,128,512]{2,1,0:T(8,128)(2,1)S(1)}, u32[]{:S(2)}, u32[]{:S(2)}) collective-permute-start(bf16[2,128,512]{2,1,0:T(8,128)(2,1)S(1)} %fusion.29), channel_id=1, source_target_pairs={{0,12},{4,16},{8,20},{12,24},{16,28},{1,13},{5,17},{9,21},{13,25},... | collective-permute-start | bytes 786440 | tf_op jit(solution)/shard_map/ppermute | solution.py:23
  69.8 4.7 %collective-permute-start.8 = (bf16[2,512,512]{2,1,0:T(8,128)(2,1)}, bf16[2,512,512]{2,1,0:T(8,128)(2,1)}, u32[]{:S(2)}, u32[]{:S(2)}) collective-permute-start(bf16[2,512,512]{2,1,0:T(8,128)(2,1)} %pad_maximum_fusion.4.kv0), channel_id=1, source_target_pairs={{0,8},{4,12},{8,16},{12,20},{16,24},{20,28},{1,9},{5,13},{9,17},{1... | collective-permute-start | bytes 3145736 | tf_op jit(solution)/shard_map/ppermute | solution.py:23
  74.6 9.7 %collective-permute-start.3 = (bf16[2,128,512]{2,1,0:T(8,128)(2,1)S(1)}, bf16[2,128,512]{2,1,0:T(8,128)(2,1)S(1)}, u32[]{:S(2)}, u32[]{:S(2)}) collective-permute-start(bf16[2,128,512]{2,1,0:T(8,128)(2,1)S(1)} %broadcast_select_fusion.5), channel_id=1, source_target_pairs={{0,24},{4,28},{1,25},{5,29},{2,26},{6,30},{3,27},{7,31}} | collective-permute-start | bytes 786440 | tf_op jit(solution)/shard_map/ppermute | solution.py:23
  86.2 9.3 %collective-permute-start.6 = (bf16[2,128,512]{2,1,0:T(8,128)(2,1)}, bf16[2,128,512]{2,1,0:T(8,128)(2,1)}, u32[]{:S(2)}, u32[]{:S(2)}) collective-permute-start(bf16[2,128,512]{2,1,0:T(8,128)(2,1)} %fusion.26), channel_id=1, source_target_pairs={{0,12},{4,16},{8,20},{12,24},{16,28},{1,13},{5,17},{9,21},{13,25},... | collective-permute-start | bytes 786440 | tf_op jit(solution)/shard_map/ppermute | solution.py:23
  95.4 6.7 %collective-permute-done.3 = bf16[2,128,512]{2,1,0:T(8,128)(2,1)S(1)} collective-permute-done((bf16[2,128,512]{2,1,0:T(8,128)(2,1)S(1)}, bf16[2,128,512]{2,1,0:T(8,128)(2,1)S(1)}, u32[]{:S(2)}, u32[]{:S(2)}) %collective-permute-start.3) | collective-permute-done | bytes 262176 | tf_op jit(solution)/shard_map/ppermute | solution.py:23
  102.3 16.0 %shard_map.76 = (bf16[512,512]{1,0:T(8,128)(2,1)}, bf16[2,512,512]{2,1,0:T(8,128)(2,1)S(1)}, bf16[2,512,512]{2,1,0:T(8,128)(2,1)}, f32[2,512,512]{2,1,0:T(8,128)...) custom-call(s32[2]{0:T(128)S(1)} %pad_add_fusion.info, bf16[512,1536]{1,0:T(8,128)(2,1)S(1)} %copy-done.18, ...), custom_call_target="tpu_custom_call" | custom-call | flops 3355443200 | bytes 8388608 | tf_op jit(solution)/shard_map/pallas_call | solution.py:111
  126.9 6.4 %collective-permute-start.7 = (bf16[2,128,512]{2,1,0:T(8,128)(2,1)S(1)}, bf16[2,128,512]{2,1,0:T(8,128)(2,1)S(1)}, u32[]{:S(2)}, u32[]{:S(2)}) collective-permute-start(bf16[2,128,512]{2,1,0:T(8,128)(2,1)S(1)} %broadcast_select_fusion.4), channel_id=1, source_target_pairs={{0,24},{4,28},{1,25},{5,29},{2,26},{6,30},{3,27},{7,31}} | collective-permute-start | bytes 786440 | tf_op jit(solution)/shard_map/ppermute | solution.py:23
  137.2 5.9 %collective-permute-done.13 = bf16[2,128,512]{2,1,0:T(8,128)(2,1)S(1)} collective-permute-done((bf16[2,128,512]{2,1,0:T(8,128)(2,1)S(1)}, bf16[2,128,512]{2,1,0:T(8,128)(2,1)S(1)}, u32[]{:S(2)}, u32[]{:S(2)}) %collective-permute-start.13) | collective-permute-done | bytes 262176 | tf_op jit(solution)/shard_map/ppermute | solution.py:23
  147.4 4.9 %collective-permute-done.9.kv1 = bf16[2,512,512]{2,1,0:T(8,128)(2,1)S(1)} collective-permute-done((bf16[2,512,512]{2,1,0:T(8,128)(2,1)S(1)}, bf16[2,512,512]{2,1,0:T(8,128)(2,1)S(1)}, u32[]{:S(2)}, u32[]{:S(2)}) %collective-permute-start.9) | collective-permute-done | bytes 1048608 | tf_op jit(solution)/shard_map/ppermute | solution.py:28
  154.9 16.0 %shard_map.77 = (bf16[512,512]{1,0:T(8,128)(2,1)}, bf16[2,512,512]{2,1,0:T(8,128)(2,1)S(1)}, bf16[2,512,512]{2,1,0:T(8,128)(2,1)}, f32[2,512,512]{2,1,0:T(8,128)...) custom-call(s32[2]{0:T(128)S(1)} %pad_add_fusion.info, bf16[512,1536]{1,0:T(8,128)(2,1)S(1)} %copy-done.19, ...), custom_call_target="tpu_custom_call" | custom-call | flops 3355443200 | bytes 8388608 | tf_op jit(solution)/shard_map/pallas_call | solution.py:111
  176.0 7.1 %collective-permute-start.11 = (bf16[2,128,512]{2,1,0:T(8,128)(2,1)}, bf16[2,128,512]{2,1,0:T(8,128)(2,1)}, u32[]{:S(2)}, u32[]{:S(2)}) collective-permute-start(bf16[2,128,512]{2,1,0:T(8,128)(2,1)} %broadcast_select_fusion.3), channel_id=1, source_target_pairs={{0,24},{4,28},{1,25},{5,29},{2,26},{6,30},{3,27},{7,31}} | collective-permute-start | bytes 786440 | tf_op jit(solution)/shard_map/ppermute | solution.py:23
  183.1 3.5 %all-to-all-start.1 = ((bf16[4,128,512]{2,1,0:T(8,128)(2,1)}), bf16[4,128,512]{2,1,0:T(8,128)(2,1)S(1)}, u32[]{:S(2)}, u32[]{:S(2)}) async-start(bf16[4,128,512]{2,1,0:T(8,128)(2,1)} %bitcast.12), calls=%async_computation.1 | async-start | bytes 1048576 | tf_op jit(solution)/shard_map/all_to_all | solution.py:227
  193.2 15.9 %shard_map.78 = (bf16[512,512]{1,0:T(8,128)(2,1)S(1)}, bf16[2,512,512]{2,1,0:T(8,128)(2,1)S(1)}, bf16[2,512,512]{2,1,0:T(8,128)(2,1)}, f32[2,512,512]{2,1,0:T(8,...) custom-call(s32[2]{0:T(128)S(1)} %pad_add_fusion.info, bf16[512,1536]{1,0:T(8,128)(2,1)S(1)} %copy-done.20, ...), custom_call_target="tpu_custom_call" | custom-call | flops 3355443200 | bytes 8388608 | tf_op jit(solution)/shard_map/pallas_call | solution.py:111
  216.8 4.8 %collective-permute-done.20 = bf16[2,128,512]{2,1,0:T(8,128)(2,1)S(1)} collective-permute-done((bf16[2,128,512]{2,1,0:T(8,128)(2,1)S(1)}, bf16[2,128,512]{2,1,0:T(8,128)(2,1)S(1)}, u32[]{:S(2)}, u32[]{:S(2)}) %collective-permute-start.20) | collective-permute-done | bytes 262176 | tf_op jit(solution)/shard_map/ppermute | solution.py:23
  225.6 8.1 %collective-permute-done.21 = bf16[2,128,512]{2,1,0:T(8,128)(2,1)S(1)} collective-permute-done((bf16[2,128,512]{2,1,0:T(8,128)(2,1)S(1)}, bf16[2,128,512]{2,1,0:T(8,128)(2,1)S(1)}, u32[]{:S(2)}, u32[]{:S(2)}) %collective-permute-start.21) | collective-permute-done | bytes 262176 | tf_op jit(solution)/shard_map/ppermute | solution.py:23
  237.4 3.5 %collective-permute-start.22 = (bf16[2,512,512]{2,1,0:T(8,128)(2,1)}, bf16[2,512,512]{2,1,0:T(8,128)(2,1)}, u32[]{:S(2)}, u32[]{:S(2)}) collective-permute-start(bf16[2,512,512]{2,1,0:T(8,128)(2,1)} %fusion.19), channel_id=1, source_target_pairs={{0,4},{4,0},{8,12},{12,8},{16,20},{20,16},{24,28},{28,24},{1,5},{5... | collective-permute-start | bytes 3145736 | tf_op jit(solution)/shard_map/ppermute | solution.py:28
  240.9 4.1 %all-to-all-start = ((bf16[4,128,512]{2,1,0:T(8,128)(2,1)}), bf16[4,128,512]{2,1,0:T(8,128)(2,1)}, u32[]{:S(2)}, u32[]{:S(2)}) async-start(bf16[4,128,512]{2,1,0:T(8,128)(2,1)} %bitcast.8), calls=%async_computation | async-start | bytes 1048576 | tf_op jit(solution)/shard_map/all_to_all | solution.py:227
  246.7 3.0 fusion.10
  251.0 2.9 all-to-all-done
  253.9 4.1 %all-to-all-start.2 = ((bf16[4,128,512]{2,1,0:T(8,128)(2,1)}), bf16[4,128,512]{2,1,0:T(8,128)(2,1)}, u32[]{:S(2)}, u32[]{:S(2)}) async-start(bf16[4,128,512]{2,1,0:T(8,128)(2,1)} %bitcast.54), calls=%async_computation.2 | async-start | bytes 1048576 | tf_op jit(solution)/shard_map/all_to_all | solution.py:227
  262.0 5.0 %all-to-all-done.2 = bf16[4,128,512]{2,1,0:T(8,128)(2,1)} async-done(((bf16[4,128,512]{2,1,0:T(8,128)(2,1)}), bf16[4,128,512]{2,1,0:T(8,128)(2,1)}, u32[]{:S(2)}, u32[]{:S(2)}) %all-to-all-start.2) | async-done | bytes 524320 | tf_op jit(solution)/shard_map/all_to_all | solution.py:227
  267.0 4.2 %all-to-all-start.3 = ((bf16[2,512,512]{2,0,1:T(2,128)(2,1)}), bf16[2,512,512]{2,0,1:T(2,128)(2,1)}, u32[]{:S(2)}, u32[]{:S(2)}) async-start(bf16[2,512,512]{2,0,1:T(2,128)(2,1)} %copy.36), calls=%async_computation.3 | async-start | bytes 2097152 | tf_op jit(solution)/shard_map/all_to_all | solution.py:214
  275.4 3.9 %collective-permute-done.19 = bf16[2,512,512]{2,1,0:T(8,128)(2,1)} collective-permute-done((bf16[2,512,512]{2,1,0:T(8,128)(2,1)}, bf16[2,512,512]{2,1,0:T(8,128)(2,1)}, u32[]{:S(2)}, u32[]{:S(2)}) %collective-permute-start.19) | collective-permute-done | bytes 1048608 | tf_op jit(solution)/shard_map/ppermute | solution.py:23
  285.8 4.2 %all-to-all-start.4 = ((bf16[2,512,512]{2,0,1:T(2,128)(2,1)}), bf16[2,512,512]{2,0,1:T(2,128)(2,1)}, u32[]{:S(2)}, u32[]{:S(2)}) async-start(bf16[2,512,512]{2,0,1:T(2,128)(2,1)} %copy.38), calls=%async_computation.4 | async-start | bytes 2097152 | tf_op jit(solution)/shard_map/all_to_all | solution.py:214
  290.2 11.6 %collective-permute-done.23 = bf16[2,512,512]{2,1,0:T(8,128)(2,1)} collective-permute-done((bf16[2,512,512]{2,1,0:T(8,128)(2,1)}, bf16[2,512,512]{2,1,0:T(8,128)(2,1)}, u32[]{:S(2)}, u32[]{:S(2)}) %collective-permute-start.23) | collective-permute-done | bytes 1048608 | tf_op jit(solution)/shard_map/ppermute | solution.py:23
  305.8 3.7 %all-to-all-start.5 = ((bf16[2,512,512]{2,0,1:T(2,128)(2,1)}), bf16[2,512,512]{2,0,1:T(2,128)(2,1)S(1)}, u32[]{:S(2)}, u32[]{:S(2)}) async-start(bf16[2,512,512]{2,0,1:T(2,128)(2,1)} %copy.40), calls=%async_computation.5 | async-start | bytes 2097152 | tf_op jit(solution)/shard_map/all_to_all | solution.py:214
  316.8 7.0 %all-to-all-done.5 = bf16[2,512,512]{2,0,1:T(2,128)(2,1)S(1)} async-done(((bf16[2,512,512]{2,0,1:T(2,128)(2,1)}), bf16[2,512,512]{2,0,1:T(2,128)(2,1)S(1)}, u32[]{:S(2)}, u32[]{:S(2)}) %all-to-all-start.5) | async-done | bytes 1048608 | tf_op jit(solution)/shard_map/all_to_all | solution.py:214
  (168 shorter events, 97.3 us)
Async XLA Ops:
  4.9 28.8 %collective-permute-start = (bf16[2,512,512]{2,1,0:T(8,128)(2,1)}, bf16[2,512,512]{2,1,0:T(8,128)(2,1)S(1)}, u32[]{:S(2)}, u32[]{:S(2)}) collective-permute-start(bf16[2,512,512]{2,1,0:T(8,128)(2,1)} %pad_maximum_fusion.2.kv0), channel_id=1, source_target_pairs={{0,8},{4,12},{8,16},{12,20},{16,24},{20,28},{1,9},{5,13},{9,17},{1... | collective-permute-start | bytes 3145736 | tf_op jit(solution)/shard_map/ppermute | solution.py:23
  10.1 46.1 %copy-start.13 = (bf16[2,512,512]{2,1,0:T(8,128)(2,1)}, bf16[2,512,512]{2,1,0:T(8,128)(2,1)S(1)}, u32[]{:S(2)}) copy-start(bf16[2,512,512]{2,1,0:T(8,128)(2,1)S(1)} %pad_maximum_fusion.3.kv0) | copy-start | bytes 3145732
  10.1 44.9 %collective-permute-start.4 = (bf16[2,512,512]{2,1,0:T(8,128)(2,1)S(1)}, bf16[2,512,512]{2,1,0:T(8,128)(2,1)S(1)}, u32[]{:S(2)}, u32[]{:S(2)}) collective-permute-start(bf16[2,512,512]{2,1,0:T(8,128)(2,1)S(1)} %pad_maximum_fusion.3.kv0), channel_id=1, source_target_pairs={{0,8},{4,12},{8,16},{12,20},{16,24},{20,28},{1,9},{5,13},{9,17},{1... | collective-permute-start | bytes 3145736 | tf_op jit(solution)/shard_map/ppermute | solution.py:23
  13.6 41.4 %copy-start.27 = (bf16[1,512,512]{2,1,0:T(8,128)(2,1)S(1)}, bf16[1,512,512]{2,1,0:T(8,128)(2,1)}, u32[]{:S(2)}) copy-start(bf16[1,512,512]{2,1,0:T(8,128)(2,1)} %copy-done.26) | copy-start | bytes 1572868
  36.4 24.7 %collective-permute-start.1 = (bf16[2,512,512]{2,1,0:T(8,128)(2,1)}, bf16[2,512,512]{2,1,0:T(8,128)(2,1)}, u32[]{:S(2)}, u32[]{:S(2)}) collective-permute-start(bf16[2,512,512]{2,1,0:T(8,128)(2,1)} %broadcast_select_fusion.2), channel_id=1, source_target_pairs={{0,4},{4,0},{8,12},{12,8},{16,20},{20,16},{24,28},{28,24},{1,5},{5... | collective-permute-start | bytes 3145736 | tf_op jit(solution)/shard_map/ppermute | solution.py:28
  56.2 28.2 %collective-permute-start.5 = (bf16[2,512,512]{2,1,0:T(8,128)(2,1)}, bf16[2,512,512]{2,1,0:T(8,128)(2,1)}, u32[]{:S(2)}, u32[]{:S(2)}) collective-permute-start(bf16[2,512,512]{2,1,0:T(8,128)(2,1)} %broadcast_select_fusion.1), channel_id=1, source_target_pairs={{0,4},{4,0},{8,12},{12,8},{16,20},{20,16},{24,28},{28,24},{1,5},{5... | collective-permute-start | bytes 3145736 | tf_op jit(solution)/shard_map/ppermute | solution.py:28
  62.4 12.2 %collective-permute-start.2 = (bf16[2,128,512]{2,1,0:T(8,128)(2,1)S(1)}, bf16[2,128,512]{2,1,0:T(8,128)(2,1)S(1)}, u32[]{:S(2)}, u32[]{:S(2)}) collective-permute-start(bf16[2,128,512]{2,1,0:T(8,128)(2,1)S(1)} %fusion.29), channel_id=1, source_target_pairs={{0,12},{4,16},{8,20},{12,24},{16,28},{1,13},{5,17},{9,21},{13,25},... | collective-permute-start | bytes 786440 | tf_op jit(solution)/shard_map/ppermute | solution.py:23
  69.8 53.0 %collective-permute-start.8 = (bf16[2,512,512]{2,1,0:T(8,128)(2,1)}, bf16[2,512,512]{2,1,0:T(8,128)(2,1)}, u32[]{:S(2)}, u32[]{:S(2)}) collective-permute-start(bf16[2,512,512]{2,1,0:T(8,128)(2,1)} %pad_maximum_fusion.4.kv0), channel_id=1, source_target_pairs={{0,8},{4,12},{8,16},{12,20},{16,24},{20,28},{1,9},{5,13},{9,17},{1... | collective-permute-start | bytes 3145736 | tf_op jit(solution)/shard_map/ppermute | solution.py:23
  74.6 27.6 %collective-permute-start.3 = (bf16[2,128,512]{2,1,0:T(8,128)(2,1)S(1)}, bf16[2,128,512]{2,1,0:T(8,128)(2,1)S(1)}, u32[]{:S(2)}, u32[]{:S(2)}) collective-permute-start(bf16[2,128,512]{2,1,0:T(8,128)(2,1)S(1)} %broadcast_select_fusion.5), channel_id=1, source_target_pairs={{0,24},{4,28},{1,25},{5,29},{2,26},{6,30},{3,27},{7,31}} | collective-permute-start | bytes 786440 | tf_op jit(solution)/shard_map/ppermute | solution.py:23
  86.2 39.8 %collective-permute-start.6 = (bf16[2,128,512]{2,1,0:T(8,128)(2,1)}, bf16[2,128,512]{2,1,0:T(8,128)(2,1)}, u32[]{:S(2)}, u32[]{:S(2)}) collective-permute-start(bf16[2,128,512]{2,1,0:T(8,128)(2,1)} %fusion.26), channel_id=1, source_target_pairs={{0,12},{4,16},{8,20},{12,24},{16,28},{1,13},{5,17},{9,21},{13,25},... | collective-permute-start | bytes 786440 | tf_op jit(solution)/shard_map/ppermute | solution.py:23
  121.5 12.2 %collective-permute-start.12 = (bf16[2,128,512]{2,1,0:T(8,128)(2,1)S(1)}, bf16[2,128,512]{2,1,0:T(8,128)(2,1)S(1)}, u32[]{:S(2)}, u32[]{:S(2)}) collective-permute-start(bf16[2,128,512]{2,1,0:T(8,128)(2,1)S(1)} %convert_element_type.121), channel_id=1, source_target_pairs={{24,0},{28,4},{25,1},{29,5},{26,2},{30,6},{27,3},{31,7}} | collective-permute-start | bytes 786440 | tf_op jit(solution)/shard_map/ppermute | solution.py:23
  123.0 29.3 %collective-permute-start.9 = (bf16[2,512,512]{2,1,0:T(8,128)(2,1)S(1)}, bf16[2,512,512]{2,1,0:T(8,128)(2,1)S(1)}, u32[]{:S(2)}, u32[]{:S(2)}) collective-permute-start(bf16[2,512,512]{2,1,0:T(8,128)(2,1)S(1)} %broadcast_select_fusion), channel_id=1, source_target_pairs={{0,4},{4,0},{8,12},{12,8},{16,20},{20,16},{24,28},{28,24},{1,5},{5... | collective-permute-start | bytes 3145736 | tf_op jit(solution)/shard_map/ppermute | solution.py:28
  126.9 10.2 %collective-permute-start.7 = (bf16[2,128,512]{2,1,0:T(8,128)(2,1)S(1)}, bf16[2,128,512]{2,1,0:T(8,128)(2,1)S(1)}, u32[]{:S(2)}, u32[]{:S(2)}) collective-permute-start(bf16[2,128,512]{2,1,0:T(8,128)(2,1)S(1)} %broadcast_select_fusion.4), channel_id=1, source_target_pairs={{0,24},{4,28},{1,25},{5,29},{2,26},{6,30},{3,27},{7,31}} | collective-permute-start | bytes 786440 | tf_op jit(solution)/shard_map/ppermute | solution.py:23
  133.8 9.3 %collective-permute-start.13 = (bf16[2,128,512]{2,1,0:T(8,128)(2,1)S(1)}, bf16[2,128,512]{2,1,0:T(8,128)(2,1)S(1)}, u32[]{:S(2)}, u32[]{:S(2)}) collective-permute-start(bf16[2,128,512]{2,1,0:T(8,128)(2,1)S(1)} %fusion.12), channel_id=1, source_target_pairs={{12,0},{16,4},{20,8},{24,12},{28,16},{13,1},{17,5},{21,9},{25,13},... | collective-permute-start | bytes 786440 | tf_op jit(solution)/shard_map/ppermute | solution.py:23
  146.1 43.1 %collective-permute-start.14 = (bf16[2,512,512]{2,1,0:T(8,128)(2,1)}, bf16[2,512,512]{2,1,0:T(8,128)(2,1)S(1)}, u32[]{:S(2)}, u32[]{:S(2)}) collective-permute-start(bf16[2,512,512]{2,1,0:T(8,128)(2,1)} %fusion.15), channel_id=1, source_target_pairs={{0,4},{4,0},{8,12},{12,8},{16,20},{20,16},{24,28},{28,24},{1,5},{5... | collective-permute-start | bytes 3145736 | tf_op jit(solution)/shard_map/ppermute | solution.py:28
  153.5 21.7 %collective-permute-start.10 = (bf16[2,128,512]{2,1,0:T(8,128)(2,1)S(1)}, bf16[2,128,512]{2,1,0:T(8,128)(2,1)S(1)}, u32[]{:S(2)}, u32[]{:S(2)}) collective-permute-start(bf16[2,128,512]{2,1,0:T(8,128)(2,1)S(1)} %fusion.23), channel_id=1, source_target_pairs={{0,12},{4,16},{8,20},{12,24},{16,28},{1,13},{5,17},{9,21},{13,25},... | collective-permute-start | bytes 786440 | tf_op jit(solution)/shard_map/ppermute | solution.py:23
  174.0 12.6 %collective-permute-start.16 = (bf16[2,128,512]{2,1,0:T(8,128)(2,1)}, bf16[2,128,512]{2,1,0:T(8,128)(2,1)S(1)}, u32[]{:S(2)}, u32[]{:S(2)}) collective-permute-start(bf16[2,128,512]{2,1,0:T(8,128)(2,1)} %convert_element_type.133), channel_id=1, source_target_pairs={{24,0},{28,4},{25,1},{29,5},{26,2},{30,6},{27,3},{31,7}} | collective-permute-start | bytes 786440 | tf_op jit(solution)/shard_map/ppermute | solution.py:23
  176.0 12.2 %collective-permute-start.11 = (bf16[2,128,512]{2,1,0:T(8,128)(2,1)}, bf16[2,128,512]{2,1,0:T(8,128)(2,1)}, u32[]{:S(2)}, u32[]{:S(2)}) collective-permute-start(bf16[2,128,512]{2,1,0:T(8,128)(2,1)} %broadcast_select_fusion.3), channel_id=1, source_target_pairs={{0,24},{4,28},{1,25},{5,29},{2,26},{6,30},{3,27},{7,31}} | collective-permute-start | bytes 786440 | tf_op jit(solution)/shard_map/ppermute | solution.py:23
  183.1 57.8 %all-to-all-start.1 = ((bf16[4,128,512]{2,1,0:T(8,128)(2,1)}), bf16[4,128,512]{2,1,0:T(8,128)(2,1)S(1)}, u32[]{:S(2)}, u32[]{:S(2)}) async-start(bf16[4,128,512]{2,1,0:T(8,128)(2,1)} %bitcast.12), calls=%async_computation.1 | async-start | bytes 1048576 | tf_op jit(solution)/shard_map/all_to_all | solution.py:227
  186.7 23.8 %collective-permute-start.17 = (bf16[2,128,512]{2,1,0:T(8,128)(2,1)S(1)}, bf16[2,128,512]{2,1,0:T(8,128)(2,1)S(1)}, u32[]{:S(2)}, u32[]{:S(2)}) collective-permute-start(bf16[2,128,512]{2,1,0:T(8,128)(2,1)S(1)} %fusion.13), channel_id=1, source_target_pairs={{12,0},{16,4},{20,8},{24,12},{28,16},{13,1},{17,5},{21,9},{25,13},... | collective-permute-start | bytes 786440 | tf_op jit(solution)/shard_map/ppermute | solution.py:23
  209.2 12.4 %collective-permute-start.20 = (bf16[2,128,512]{2,1,0:T(8,128)(2,1)S(1)}, bf16[2,128,512]{2,1,0:T(8,128)(2,1)S(1)}, u32[]{:S(2)}, u32[]{:S(2)}) collective-permute-start(bf16[2,128,512]{2,1,0:T(8,128)(2,1)S(1)} %convert_element_type.146), channel_id=1, source_target_pairs={{24,0},{28,4},{25,1},{29,5},{26,2},{30,6},{27,3},{31,7}} | collective-permute-start | bytes 786440 | tf_op jit(solution)/shard_map/ppermute | solution.py:23
  214.3 32.4 %collective-permute-start.18 = (bf16[2,512,512]{2,1,0:T(8,128)(2,1)}, bf16[2,512,512]{2,1,0:T(8,128)(2,1)}, u32[]{:S(2)}, u32[]{:S(2)}) collective-permute-start(bf16[2,512,512]{2,1,0:T(8,128)(2,1)} %fusion.17), channel_id=1, source_target_pairs={{0,4},{4,0},{8,12},{12,8},{16,20},{20,16},{24,28},{28,24},{1,5},{5... | collective-permute-start | bytes 3145736 | tf_op jit(solution)/shard_map/ppermute | solution.py:28
  221.7 12.0 %collective-permute-start.21 = (bf16[2,128,512]{2,1,0:T(8,128)(2,1)S(1)}, bf16[2,128,512]{2,1,0:T(8,128)(2,1)S(1)}, u32[]{:S(2)}, u32[]{:S(2)}) collective-permute-start(bf16[2,128,512]{2,1,0:T(8,128)(2,1)S(1)} %fusion.14), channel_id=1, source_target_pairs={{12,0},{16,4},{20,8},{24,12},{28,16},{13,1},{17,5},{21,9},{25,13},... | collective-permute-start | bytes 786440 | tf_op jit(solution)/shard_map/ppermute | solution.py:23
  224.3 34.0 %collective-permute-start.15 = (bf16[2,512,512]{2,1,0:T(8,128)(2,1)}, bf16[2,512,512]{2,1,0:T(8,128)(2,1)}, u32[]{:S(2)}, u32[]{:S(2)}) collective-permute-start(bf16[2,512,512]{2,1,0:T(8,128)(2,1)} %fusion.9), channel_id=1, source_target_pairs={{8,0},{12,4},{16,8},{20,12},{24,16},{28,20},{9,1},{13,5},{17,9},{2... | collective-permute-start | bytes 3145736 | tf_op jit(solution)/shard_map/ppermute | solution.py:23
  237.4 33.9 %collective-permute-start.22 = (bf16[2,512,512]{2,1,0:T(8,128)(2,1)}, bf16[2,512,512]{2,1,0:T(8,128)(2,1)}, u32[]{:S(2)}, u32[]{:S(2)}) collective-permute-start(bf16[2,512,512]{2,1,0:T(8,128)(2,1)} %fusion.19), channel_id=1, source_target_pairs={{0,4},{4,0},{8,12},{12,8},{16,20},{20,16},{24,28},{28,24},{1,5},{5... | collective-permute-start | bytes 3145736 | tf_op jit(solution)/shard_map/ppermute | solution.py:28
  240.9 13.1 %all-to-all-start = ((bf16[4,128,512]{2,1,0:T(8,128)(2,1)}), bf16[4,128,512]{2,1,0:T(8,128)(2,1)}, u32[]{:S(2)}, u32[]{:S(2)}) async-start(bf16[4,128,512]{2,1,0:T(8,128)(2,1)} %bitcast.8), calls=%async_computation | async-start | bytes 1048576 | tf_op jit(solution)/shard_map/all_to_all | solution.py:227
  249.7 29.6 %collective-permute-start.19 = (bf16[2,512,512]{2,1,0:T(8,128)(2,1)}, bf16[2,512,512]{2,1,0:T(8,128)(2,1)}, u32[]{:S(2)}, u32[]{:S(2)}) collective-permute-start(bf16[2,512,512]{2,1,0:T(8,128)(2,1)} %fusion.10), channel_id=1, source_target_pairs={{8,0},{12,4},{16,8},{20,12},{24,16},{28,20},{9,1},{13,5},{17,9},{2... | collective-permute-start | bytes 3145736 | tf_op jit(solution)/shard_map/ppermute | solution.py:23
  253.9 13.1 %all-to-all-start.2 = ((bf16[4,128,512]{2,1,0:T(8,128)(2,1)}), bf16[4,128,512]{2,1,0:T(8,128)(2,1)}, u32[]{:S(2)}, u32[]{:S(2)}) async-start(bf16[4,128,512]{2,1,0:T(8,128)(2,1)} %bitcast.54), calls=%async_computation.2 | async-start | bytes 1048576 | tf_op jit(solution)/shard_map/all_to_all | solution.py:227
  267.0 18.8 %all-to-all-start.3 = ((bf16[2,512,512]{2,0,1:T(2,128)(2,1)}), bf16[2,512,512]{2,0,1:T(2,128)(2,1)}, u32[]{:S(2)}, u32[]{:S(2)}) async-start(bf16[2,512,512]{2,0,1:T(2,128)(2,1)} %copy.36), calls=%async_computation.3 | async-start | bytes 2097152 | tf_op jit(solution)/shard_map/all_to_all | solution.py:214
  273.9 27.8 %collective-permute-start.23 = (bf16[2,512,512]{2,1,0:T(8,128)(2,1)}, bf16[2,512,512]{2,1,0:T(8,128)(2,1)}, u32[]{:S(2)}, u32[]{:S(2)}) collective-permute-start(bf16[2,512,512]{2,1,0:T(8,128)(2,1)} %fusion.11), channel_id=1, source_target_pairs={{8,0},{12,4},{16,8},{20,12},{24,16},{28,20},{9,1},{13,5},{17,9},{2... | collective-permute-start | bytes 3145736 | tf_op jit(solution)/shard_map/ppermute | solution.py:23
  285.8 20.1 %all-to-all-start.4 = ((bf16[2,512,512]{2,0,1:T(2,128)(2,1)}), bf16[2,512,512]{2,0,1:T(2,128)(2,1)}, u32[]{:S(2)}, u32[]{:S(2)}) async-start(bf16[2,512,512]{2,0,1:T(2,128)(2,1)} %copy.38), calls=%async_computation.4 | async-start | bytes 2097152 | tf_op jit(solution)/shard_map/all_to_all | solution.py:214
  305.8 18.0 %all-to-all-start.5 = ((bf16[2,512,512]{2,0,1:T(2,128)(2,1)}), bf16[2,512,512]{2,0,1:T(2,128)(2,1)S(1)}, u32[]{:S(2)}, u32[]{:S(2)}) async-start(bf16[2,512,512]{2,0,1:T(2,128)(2,1)} %copy.40), calls=%async_computation.5 | async-start | bytes 2097152 | tf_op jit(solution)/shard_map/all_to_all | solution.py:214
  (39 other events, 484.9 us)

commit v3 on v2

--- a/solution.py
+++ b/solution.py
@@ -14,7 +14,7 @@
 STRIDE = 32
 REACH = 2
 PAIR = 2 * BLOCK
-CHUNKS = 3
+CHUNKS = 2
 
 
 def shifted(value, axis, steps):
@@ -174,7 +174,8 @@
         stacked.append((kv0, shifted(kv0, "ctx", 2)))
 
     def gathered(kv0, kv2, here):
-        kv1 = swapped(jnp.where(here % 2 == 1, kv2, kv0), "ctx")
+        kv1 = swapped(jnp.where(odd, kv2, kv0), "ctx")
+        away = here - owner
         tiles = []
         for s in range(n_sum):
             at = (0, local_start[s], 0)
@@ -183,7 +184,7 @@
             near = lax.dynamic_slice(kv1, at, size)
             own = lax.dynamic_slice(kv0, at, size)
             tiles.append(
-                jnp.where(distance[s] == 2, far, jnp.where(distance[s] == 1, near, own))
+                jnp.where(away[s] == 2, far, jnp.where(away[s] == 1, near, own))
             )
         kvs = jnp.concatenate(tiles, axis=1)
         for jump in jumps:
@@ -211,22 +212,22 @@
         p2 = jnp.where(odd, p2.astype(jnp.float32) + wide, p2.astype(jnp.float32))
         far = shifted(p2.astype(jnp.bfloat16), "ctx", -2).astype(jnp.float32)
         total = (p0 + jnp.where(odd, 0.0, wide) + far).astype(jnp.bfloat16)
-        return near, lax.all_to_all(total, "tp", split_axis=1, concat_axis=2, tiled=True)
+        return ps, lax.all_to_all(total, "tp", split_axis=1, concat_axis=2, tiled=True)
 
     grads = []
     tokens = []
     returns = []
     for chunk in range(CHUNKS):
-        here = tokens[chunk - 2][0] if chunk >= 2 else me
-        after = returns[chunk - 2] if chunk >= 2 else summary_offset
+        here = tokens[chunk - 1][0] if chunk >= 1 else me
+        after = returns[chunk - 1] if chunk >= 1 else summary_offset
         ready = gathered(*stacked[chunk], here)
         gq, p2, p1, p0, ps, token = attention(
             info, query, dout, *ready, after, chunk * heads, n_sum
         )
         tokens.append(token)
         moved_q = lax.all_to_all(gq, "tp", split_axis=0, concat_axis=1, tiled=True)
-        near, moved_kv = returned(p2, p1, p0, ps)
-        returns.append(near)
+        summed, moved_kv = returned(p2, p1, p0, ps)
+        returns.append(summed)
         grads.append((moved_q, moved_kv[0], moved_kv[1]))
 
     def joined(pieces):

time: 333 us -> 361 us (1.084)
  waiting for transfers between devices: 107 us -> 181 us
  starting transfers between devices: 101 us -> 82.5 us
  other arithmetic: 39.7 us -> 27.6 us
  local copies, waits for them, and re-layouts: 31.6 us -> 20 us
    ppermute x6 -> x4, waiting for transfers between devices: 9.27 us -> 64.5 us  [swapped(): lax.ppermute(value, axis, [(source, source ^ 1) for source in range(count)])]
    ppermute x18 -> x12, waiting for transfers between devices: 80.7 us -> 96.5 us  [shifted(): lax.ppermute(value, axis, [(source, source + steps) for source in range(l...]
    unnamed x84 -> x34, local copies, waits for them, and re-layouts: 13.6 us -> 5.5 us
    all_to_all x3 -> x2, waiting for transfers between devices: 9.32 us -> 16.1 us  [returned(): lax.all_to_all(total, 'tp', split_axis=1, concat_axis=2, tiled=True)]
    all_to_all x3 -> x2, starting transfers between devices: 12.2 us -> 7.13 us  [returned(): lax.all_to_all(total, 'tp', split_axis=1, concat_axis=2, tiled=True)]
    ppermute x18 -> x12, starting transfers between devices: 63.7 us -> 58.8 us  [shifted(): lax.ppermute(value, axis, [(source, source + steps) for source in range(l...]
    ppermute x6 -> x4, starting transfers between devices: 13.3 us -> 8.47 us  [swapped(): lax.ppermute(value, axis, [(source, source ^ 1) for source in range(count)])]
    all_to_all x3 -> x2, waiting for transfers between devices: 7.92 us -> 3.66 us  [on_device(): moved_q = lax.all_to_all(gq, 'tp', split_axis=0, concat_axis=1, tiled=True)]
  transfers between devices with their start and end apart: 30 -> 20, of which waited for: 17 -> 15; matrix products, arithmetic and copies ran while one was open for 15% -> 9% of each run, Pallas kernels for 14% -> 6%
where the time goes in v3:
time: 361 us; the launch traced here: 360 us
  waiting for transfers between devices  181 us (50%)
  starting transfers between devices  82.5 us (23%)
  Pallas kernels  46.3 us (13%)
  other arithmetic  27.6 us (8%)
  local copies, waits for them, and re-layouts  20 us (6%)
    ppermute x12, waiting for transfers between devices, shifted(): lax.ppermute(value, axis, [(source, source + steps) for source in range(l...  96.5 us
    ppermute x4, waiting for transfers between devices, swapped(): lax.ppermute(value, axis, [(source, source ^ 1) for source in range(count)])  64.5 us
    ppermute x12, starting transfers between devices, shifted(): lax.ppermute(value, axis, [(source, source + steps) for source in range(l...  58.8 us
    pallas_call x2, Pallas kernels, attention(): pl.pallas_call(functools.partial(attend, n_sum), grid=(heads,), in_specs=...  46.3 us
    all_to_all x2, waiting for transfers between devices, returned(): lax.all_to_all(total, 'tp', split_axis=1, concat_axis=2, tiled=True)  16.1 us
    ppermute x4, starting transfers between devices, swapped(): lax.ppermute(value, axis, [(source, source ^ 1) for source in range(count)])  8.47 us
    all_to_all x2, starting transfers between devices, on_device(): moved_q = lax.all_to_all(gq, 'tp', split_axis=0, concat_axis=1, tiled=True)  8.04 us
  transfers between devices with their start and end apart: 20, of which 15 were waited for; matrix products, arithmetic and copies ran while one was open for 9% of the time, Pallas kernels for 6%

profile of v3, /device:TPU:0, one launch (start us, length us, event | category | flops | bytes accessed | tf_op | source)
XLA Modules:
  0.0 359.6 jit_solution(12710124376036641383)
XLA Ops:
  0.6 3.2 slice_bitcast_fusion.6
  5.0 5.0 %collective-permute-start = (bf16[2,512,768]{2,1,0:T(8,128)(2,1)S(1)}, bf16[2,512,768]{2,1,0:T(8,128)(2,1)S(1)}, u32[]{:S(2)}, u32[]{:S(2)}) collective-permute-start(bf16[2,512,768]{2,1,0:T(8,128)(2,1)S(1)} %pad_maximum_fusion.kv0), channel_id=1, source_target_pairs={{0,8},{4,12},{8,16},{12,20},{16,24},{20,28},{1,9},{5,13},{9,17},{1... | collective-permute-start | bytes 4718600 | tf_op jit(solution)/shard_map/ppermute | solution.py:23
  10.1 33.5 %collective-permute-done.kv2 = bf16[2,512,768]{2,1,0:T(8,128)(2,1)S(1)} collective-permute-done((bf16[2,512,768]{2,1,0:T(8,128)(2,1)S(1)}, bf16[2,512,768]{2,1,0:T(8,128)(2,1)S(1)}, u32[]{:S(2)}, u32[]{:S(2)}) %collective-permute-start) | collective-permute-done | bytes 1572896 | tf_op jit(solution)/shard_map/ppermute | solution.py:23
  49.1 4.5 %collective-permute-start.4 = (bf16[2,512,768]{2,1,0:T(8,128)(2,1)}, bf16[2,512,768]{2,1,0:T(8,128)(2,1)S(1)}, u32[]{:S(2)}, u32[]{:S(2)}) collective-permute-start(bf16[2,512,768]{2,1,0:T(8,128)(2,1)} %pad_maximum_fusion.1.kv0), channel_id=1, source_target_pairs={{0,8},{4,12},{8,16},{12,20},{16,24},{20,28},{1,9},{5,13},{9,17},{1... | collective-permute-start | bytes 4718600 | tf_op jit(solution)/shard_map/ppermute | solution.py:23
  54.3 27.6 %collective-permute-done.1.kv1 = bf16[2,512,768]{2,1,0:T(8,128)(2,1)} collective-permute-done((bf16[2,512,768]{2,1,0:T(8,128)(2,1)}, bf16[2,512,768]{2,1,0:T(8,128)(2,1)}, u32[]{:S(2)}, u32[]{:S(2)}) %collective-permute-start.1) | collective-permute-done | bytes 1572896 | tf_op jit(solution)/shard_map/ppermute | solution.py:28
  83.2 5.4 %collective-permute-start.2 = (bf16[2,128,768]{2,1,0:T(8,128)(2,1)S(1)}, bf16[2,128,768]{2,1,0:T(8,128)(2,1)S(1)}, u32[]{:S(2)}, u32[]{:S(2)}) collective-permute-start(bf16[2,128,768]{2,1,0:T(8,128)(2,1)S(1)} %fusion.19), channel_id=1, source_target_pairs={{0,12},{4,16},{8,20},{12,24},{16,28},{1,13},{5,17},{9,21},{13,25},... | collective-permute-start | bytes 1179656 | tf_op jit(solution)/shard_map/ppermute | solution.py:23
  90.5 4.7 %collective-permute-done.2 = bf16[2,128,768]{2,1,0:T(8,128)(2,1)S(1)} collective-permute-done((bf16[2,128,768]{2,1,0:T(8,128)(2,1)S(1)}, bf16[2,128,768]{2,1,0:T(8,128)(2,1)S(1)}, u32[]{:S(2)}, u32[]{:S(2)}) %collective-permute-start.2) | collective-permute-done | bytes 393248 | tf_op jit(solution)/shard_map/ppermute | solution.py:23
  95.2 24.1 %collective-permute-start.3 = (bf16[2,128,768]{2,1,0:T(8,128)(2,1)S(1)}, bf16[2,128,768]{2,1,0:T(8,128)(2,1)S(1)}, u32[]{:S(2)}, u32[]{:S(2)}) collective-permute-start(bf16[2,128,768]{2,1,0:T(8,128)(2,1)S(1)} %broadcast_select_fusion.3), channel_id=1, source_target_pairs={{0,24},{4,28},{1,25},{5,29},{2,26},{6,30},{3,27},{7,31}} | collective-permute-start | bytes 1179656 | tf_op jit(solution)/shard_map/ppermute | solution.py:23
  119.5 8.3 %collective-permute-done.3 = bf16[2,128,768]{2,1,0:T(8,128)(2,1)S(1)} collective-permute-done((bf16[2,128,768]{2,1,0:T(8,128)(2,1)S(1)}, bf16[2,128,768]{2,1,0:T(8,128)(2,1)S(1)}, u32[]{:S(2)}, u32[]{:S(2)}) %collective-permute-start.3) | collective-permute-done | bytes 393248 | tf_op jit(solution)/shard_map/ppermute | solution.py:23
  127.8 23.2 %shard_map.76 = (bf16[512,768]{1,0:T(8,128)(2,1)}, bf16[2,512,768]{2,1,0:T(8,128)(2,1)S(1)}, bf16[2,512,768]{2,1,0:T(8,128)(2,1)S(1)}, f32[2,512,768]{2,1,0:T(8,...) custom-call(s32[2]{0:T(128)S(1)} %pad_add_fusion.info, bf16[512,1536]{1,0:T(8,128)(2,1)S(1)} %copy-done.4, ...), custom_call_target="tpu_custom_call" | custom-call | flops 5033164800 | bytes 12582912 | tf_op jit(solution)/shard_map/pallas_call | solution.py:111
  154.5 6.4 %collective-permute-done.6 = bf16[2,128,768]{2,1,0:T(8,128)(2,1)S(1)} collective-permute-done((bf16[2,128,768]{2,1,0:T(8,128)(2,1)S(1)}, bf16[2,128,768]{2,1,0:T(8,128)(2,1)S(1)}, u32[]{:S(2)}, u32[]{:S(2)}) %collective-permute-start.6) | collective-permute-done | bytes 393248 | tf_op jit(solution)/shard_map/ppermute | solution.py:23
  161.0 10.8 %collective-permute-start.7 = (bf16[2,128,768]{2,1,0:T(8,128)(2,1)S(1)}, bf16[2,128,768]{2,1,0:T(8,128)(2,1)S(1)}, u32[]{:S(2)}, u32[]{:S(2)}) collective-permute-start(bf16[2,128,768]{2,1,0:T(8,128)(2,1)S(1)} %broadcast_select_fusion.2), channel_id=1, source_target_pairs={{0,24},{4,28},{1,25},{5,29},{2,26},{6,30},{3,27},{7,31}} | collective-permute-start | bytes 1179656 | tf_op jit(solution)/shard_map/ppermute | solution.py:23
  173.3 5.2 %collective-permute-done.7 = bf16[2,128,768]{2,1,0:T(8,128)(2,1)S(1)} collective-permute-done((bf16[2,128,768]{2,1,0:T(8,128)(2,1)S(1)}, bf16[2,128,768]{2,1,0:T(8,128)(2,1)S(1)}, u32[]{:S(2)}, u32[]{:S(2)}) %collective-permute-start.7) | collective-permute-done | bytes 393248 | tf_op jit(solution)/shard_map/ppermute | solution.py:23
  178.5 5.1 %collective-permute-done.9 = bf16[2,128,768]{2,1,0:T(8,128)(2,1)S(1)} collective-permute-done((bf16[2,128,768]{2,1,0:T(8,128)(2,1)S(1)}, bf16[2,128,768]{2,1,0:T(8,128)(2,1)S(1)}, u32[]{:S(2)}, u32[]{:S(2)}) %collective-permute-start.9) | collective-permute-done | bytes 393248 | tf_op jit(solution)/shard_map/ppermute | solution.py:23
  183.8 23.1 %shard_map.77 = (bf16[512,768]{1,0:T(8,128)(2,1)}, bf16[2,512,768]{2,1,0:T(8,128)(2,1)S(1)}, bf16[2,512,768]{2,1,0:T(8,128)(2,1)}, f32[2,512,768]{2,1,0:T(8,128)}, f32[2,128,768]{2,1,0:T(8,128)S(1)}, /*index=5*/s32[1]{0:T(128)}) custom-call(s32[2]{0:T(128)S(1)} %pad_add_fusion.info, bf16[512,1536]{1,0:T(8,128)(2,1)S(1)} %copy-done.4, ...), custom_call_target="tpu_custom_call" | custom-call | flops 5033164800 | bytes 12582912 | tf_op jit(solution)/shard_map/pallas_call | solution.py:111
  208.5 12.4 %collective-permute-done.12 = bf16[2,128,768]{2,1,0:T(8,128)(2,1)S(1)} collective-permute-done((bf16[2,128,768]{2,1,0:T(8,128)(2,1)S(1)}, bf16[2,128,768]{2,1,0:T(8,128)(2,1)S(1)}, u32[]{:S(2)}, u32[]{:S(2)}) %collective-permute-start.12) | collective-permute-done | bytes 393248 | tf_op jit(solution)/shard_map/ppermute | solution.py:23
  222.3 9.4 %collective-permute-done.13 = bf16[2,128,768]{2,1,0:T(8,128)(2,1)S(1)} collective-permute-done((bf16[2,128,768]{2,1,0:T(8,128)(2,1)S(1)}, bf16[2,128,768]{2,1,0:T(8,128)(2,1)S(1)}, u32[]{:S(2)}, u32[]{:S(2)}) %collective-permute-start.13) | collective-permute-done | bytes 393248 | tf_op jit(solution)/shard_map/ppermute | solution.py:23
  234.1 5.3 %collective-permute-start.14 = (bf16[2,512,768]{2,1,0:T(8,128)(2,1)}, bf16[2,512,768]{2,1,0:T(8,128)(2,1)}, u32[]{:S(2)}, u32[]{:S(2)}) collective-permute-start(bf16[2,512,768]{2,1,0:T(8,128)(2,1)} %fusion.12), channel_id=1, source_target_pairs={{0,4},{4,0},{8,12},{12,8},{16,20},{20,16},{24,28},{28,24},{1,5},{5... | collective-permute-start | bytes 4718600 | tf_op jit(solution)/shard_map/ppermute | solution.py:28
  239.4 14.8 %collective-permute-done.10 = bf16[2,512,768]{2,1,0:T(8,128)(2,1)S(1)} collective-permute-done((bf16[2,512,768]{2,1,0:T(8,128)(2,1)S(1)}, bf16[2,512,768]{2,1,0:T(8,128)(2,1)S(1)}, u32[]{:S(2)}, u32[]{:S(2)}) %collective-permute-start.10) | collective-permute-done | bytes 1572896 | tf_op jit(solution)/shard_map/ppermute | solution.py:28
  257.2 4.5 %all-to-all-start = ((bf16[4,128,768]{2,1,0:T(8,128)(2,1)}), bf16[4,128,768]{2,1,0:T(8,128)(2,1)}, u32[]{:S(2)}, u32[]{:S(2)}) async-start(bf16[4,128,768]{2,1,0:T(8,128)(2,1)} %bitcast.8), calls=%async_computation | async-start | bytes 1572864 | tf_op jit(solution)/shard_map/all_to_all | solution.py:228
  261.7 22.1 %collective-permute-done.14 = bf16[2,512,768]{2,1,0:T(8,128)(2,1)} collective-permute-done((bf16[2,512,768]{2,1,0:T(8,128)(2,1)}, bf16[2,512,768]{2,1,0:T(8,128)(2,1)}, u32[]{:S(2)}, u32[]{:S(2)}) %collective-permute-start.14) | collective-permute-done | bytes 1572896 | tf_op jit(solution)/shard_map/ppermute | solution.py:28
  283.9 3.0 fusion.7
  288.2 3.5 all-to-all-start.1
  294.0 2.9 fusion.2
  296.9 2.8 copy.31
  299.7 3.7 %all-to-all-done.1 = bf16[4,128,768]{2,1,0:T(8,128)(2,1)S(1)} async-done(((bf16[4,128,768]{2,1,0:T(8,128)(2,1)}), bf16[4,128,768]{2,1,0:T(8,128)(2,1)S(1)}, u32[]{:S(2)}, u32[]{:S(2)}) %all-to-all-start.1) | async-done | bytes 786464 | tf_op jit(solution)/shard_map/all_to_all | solution.py:228
  304.2 3.6 all-to-all-start.2
  309.9 11.4 %collective-permute-done.15 = bf16[2,512,768]{2,1,0:T(8,128)(2,1)} collective-permute-done((bf16[2,512,768]{2,1,0:T(8,128)(2,1)}, bf16[2,512,768]{2,1,0:T(8,128)(2,1)}, u32[]{:S(2)}, u32[]{:S(2)}) %collective-permute-start.15) | collective-permute-done | bytes 1572896 | tf_op jit(solution)/shard_map/ppermute | solution.py:23
  321.3 3.4 fusion.5
  324.8 2.8 copy.33
  327.8 3.6 all-to-all-start.3
  335.7 15.8 %all-to-all-done.3 = bf16[2,512,768]{2,0,1:T(2,128)(2,1)S(1)} async-done(((bf16[2,512,768]{2,0,1:T(2,128)(2,1)}), bf16[2,512,768]{2,0,1:T(2,128)(2,1)S(1)}, u32[]{:S(2)}, u32[]{:S(2)}) %all-to-all-start.3) | async-done | bytes 1572896 | tf_op jit(solution)/shard_map/all_to_all | solution.py:215
  (82 shorter events, 42.1 us)
Async XLA Ops:
  5.0 41.3 %copy-start.2 = (bf16[2,512,768]{2,1,0:T(8,128)(2,1)}, bf16[2,512,768]{2,1,0:T(8,128)(2,1)S(1)}, u32[]{:S(2)}) copy-start(bf16[2,512,768]{2,1,0:T(8,128)(2,1)S(1)} %pad_maximum_fusion.kv0) | copy-start | bytes 4718596
  5.0 38.6 %collective-permute-start = (bf16[2,512,768]{2,1,0:T(8,128)(2,1)S(1)}, bf16[2,512,768]{2,1,0:T(8,128)(2,1)S(1)}, u32[]{:S(2)}, u32[]{:S(2)}) collective-permute-start(bf16[2,512,768]{2,1,0:T(8,128)(2,1)S(1)} %pad_maximum_fusion.kv0), channel_id=1, source_target_pairs={{0,8},{4,12},{8,16},{12,20},{16,24},{20,28},{1,9},{5,13},{9,17},{1... | collective-permute-start | bytes 4718600 | tf_op jit(solution)/shard_map/ppermute | solution.py:23
  10.1 37.8 %copy-start.6 = (bf16[1,512,768]{2,1,0:T(8,128)(2,1)S(1)}, bf16[1,512,768]{2,1,0:T(8,128)(2,1)}, u32[]{:S(2)}) copy-start(bf16[1,512,768]{2,1,0:T(8,128)(2,1)} %get-tuple-element.42) | copy-start | bytes 2359300
  10.1 37.8 %copy-start.8 = (bf16[1,512,768]{2,1,0:T(8,128)(2,1)S(1)}, bf16[1,512,768]{2,1,0:T(8,128)(2,1)}, u32[]{:S(2)}) copy-start(bf16[1,512,768]{2,1,0:T(8,128)(2,1)} %get-tuple-element.43) | copy-start | bytes 2359300
  46.3 35.6 %collective-permute-start.1 = (bf16[2,512,768]{2,1,0:T(8,128)(2,1)}, bf16[2,512,768]{2,1,0:T(8,128)(2,1)}, u32[]{:S(2)}, u32[]{:S(2)}) collective-permute-start(bf16[2,512,768]{2,1,0:T(8,128)(2,1)} %broadcast_select_fusion.1), channel_id=1, source_target_pairs={{0,4},{4,0},{8,12},{12,8},{16,20},{20,16},{24,28},{28,24},{1,5},{5... | collective-permute-start | bytes 4718600 | tf_op jit(solution)/shard_map/ppermute | solution.py:28
  49.1 39.5 %collective-permute-start.4 = (bf16[2,512,768]{2,1,0:T(8,128)(2,1)}, bf16[2,512,768]{2,1,0:T(8,128)(2,1)S(1)}, u32[]{:S(2)}, u32[]{:S(2)}) collective-permute-start(bf16[2,512,768]{2,1,0:T(8,128)(2,1)} %pad_maximum_fusion.1.kv0), channel_id=1, source_target_pairs={{0,8},{4,12},{8,16},{12,20},{16,24},{20,28},{1,9},{5,13},{9,17},{1... | collective-permute-start | bytes 4718600 | tf_op jit(solution)/shard_map/ppermute | solution.py:23
  54.3 34.3 %copy-start.7 = (bf16[1,512,768]{2,1,0:T(8,128)(2,1)S(1)}, bf16[1,512,768]{2,1,0:T(8,128)(2,1)}, u32[]{:S(2)}) copy-start(bf16[1,512,768]{2,1,0:T(8,128)(2,1)} %get-tuple-element.42) | copy-start | bytes 2359300
  54.3 34.3 %copy-start.9 = (bf16[1,512,768]{2,1,0:T(8,128)(2,1)S(1)}, bf16[1,512,768]{2,1,0:T(8,128)(2,1)}, u32[]{:S(2)}) copy-start(bf16[1,512,768]{2,1,0:T(8,128)(2,1)} %get-tuple-element.43) | copy-start | bytes 2359300
  83.2 12.0 %collective-permute-start.2 = (bf16[2,128,768]{2,1,0:T(8,128)(2,1)S(1)}, bf16[2,128,768]{2,1,0:T(8,128)(2,1)S(1)}, u32[]{:S(2)}, u32[]{:S(2)}) collective-permute-start(bf16[2,128,768]{2,1,0:T(8,128)(2,1)S(1)} %fusion.19), channel_id=1, source_target_pairs={{0,12},{4,16},{8,20},{12,24},{16,28},{1,13},{5,17},{9,21},{13,25},... | collective-permute-start | bytes 1179656 | tf_op jit(solution)/shard_map/ppermute | solution.py:23
  88.6 39.2 %copy-start.4 = (bf16[512,1536]{1,0:T(8,128)(2,1)S(1)}, bf16[512,1536]{1,0:T(8,128)(2,1)}, u32[]{:S(2)}) copy-start(bf16[512,1536]{1,0:T(8,128)(2,1)} %q.3) | copy-start | bytes 4718596
  88.6 39.2 %copy-start.5 = (bf16[512,1536]{1,0:T(8,128)(2,1)S(1)}, bf16[512,1536]{1,0:T(8,128)(2,1)}, u32[]{:S(2)}) copy-start(bf16[512,1536]{1,0:T(8,128)(2,1)} %do.3) | copy-start | bytes 4718596
  88.9 38.9 %copy-start.3 = (bf16[2,512,768]{2,1,0:T(8,128)(2,1)S(1)}, bf16[2,512,768]{2,1,0:T(8,128)(2,1)}, u32[]{:S(2)}) copy-start(bf16[2,512,768]{2,1,0:T(8,128)(2,1)} %copy-done.2) | copy-start | bytes 4718596
  88.9 62.8 %collective-permute-start.5 = (bf16[2,512,768]{2,1,0:T(8,128)(2,1)S(1)}, bf16[2,512,768]{2,1,0:T(8,128)(2,1)S(1)}, u32[]{:S(2)}, u32[]{:S(2)}) collective-permute-start(bf16[2,512,768]{2,1,0:T(8,128)(2,1)S(1)} %broadcast_select_fusion), channel_id=1, source_target_pairs={{0,4},{4,0},{8,12},{12,8},{16,20},{20,16},{24,28},{28,24},{1,5},{5... | collective-permute-start | bytes 4718600 | tf_op jit(solution)/shard_map/ppermute | solution.py:28
  95.2 32.5 %collective-permute-start.3 = (bf16[2,128,768]{2,1,0:T(8,128)(2,1)S(1)}, bf16[2,128,768]{2,1,0:T(8,128)(2,1)S(1)}, u32[]{:S(2)}, u32[]{:S(2)}) collective-permute-start(bf16[2,128,768]{2,1,0:T(8,128)(2,1)S(1)} %broadcast_select_fusion.3), channel_id=1, source_target_pairs={{0,24},{4,28},{1,25},{5,29},{2,26},{6,30},{3,27},{7,31}} | collective-permute-start | bytes 1179656 | tf_op jit(solution)/shard_map/ppermute | solution.py:23
  151.8 9.1 %collective-permute-start.6 = (bf16[2,128,768]{2,1,0:T(8,128)(2,1)S(1)}, bf16[2,128,768]{2,1,0:T(8,128)(2,1)S(1)}, u32[]{:S(2)}, u32[]{:S(2)}) collective-permute-start(bf16[2,128,768]{2,1,0:T(8,128)(2,1)S(1)} %fusion.16), channel_id=1, source_target_pairs={{0,12},{4,16},{8,20},{12,24},{16,28},{1,13},{5,17},{9,21},{13,25},... | collective-permute-start | bytes 1179656 | tf_op jit(solution)/shard_map/ppermute | solution.py:23
  153.2 18.6 %collective-permute-start.8 = (bf16[2,128,768]{2,1,0:T(8,128)(2,1)S(1)}, bf16[2,128,768]{2,1,0:T(8,128)(2,1)S(1)}, u32[]{:S(2)}, u32[]{:S(2)}) collective-permute-start(bf16[2,128,768]{2,1,0:T(8,128)(2,1)S(1)} %convert_element_type.80), channel_id=1, source_target_pairs={{24,0},{28,4},{25,1},{29,5},{26,2},{30,6},{27,3},{31,7}} | collective-permute-start | bytes 1179656 | tf_op jit(solution)/shard_map/ppermute | solution.py:23
  161.0 17.4 %collective-permute-start.7 = (bf16[2,128,768]{2,1,0:T(8,128)(2,1)S(1)}, bf16[2,128,768]{2,1,0:T(8,128)(2,1)S(1)}, u32[]{:S(2)}, u32[]{:S(2)}) collective-permute-start(bf16[2,128,768]{2,1,0:T(8,128)(2,1)S(1)} %broadcast_select_fusion.2), channel_id=1, source_target_pairs={{0,24},{4,28},{1,25},{5,29},{2,26},{6,30},{3,27},{7,31}} | collective-permute-start | bytes 1179656 | tf_op jit(solution)/shard_map/ppermute | solution.py:23
  171.9 11.6 %collective-permute-start.9 = (bf16[2,128,768]{2,1,0:T(8,128)(2,1)S(1)}, bf16[2,128,768]{2,1,0:T(8,128)(2,1)S(1)}, u32[]{:S(2)}, u32[]{:S(2)}) collective-permute-start(bf16[2,128,768]{2,1,0:T(8,128)(2,1)S(1)} %fusion.8), channel_id=1, source_target_pairs={{12,0},{16,4},{20,8},{24,12},{28,16},{13,1},{17,5},{21,9},{25,13},... | collective-permute-start | bytes 1179656 | tf_op jit(solution)/shard_map/ppermute | solution.py:23
  207.0 13.9 %collective-permute-start.12 = (bf16[2,128,768]{2,1,0:T(8,128)(2,1)S(1)}, bf16[2,128,768]{2,1,0:T(8,128)(2,1)S(1)}, u32[]{:S(2)}, u32[]{:S(2)}) collective-permute-start(bf16[2,128,768]{2,1,0:T(8,128)(2,1)S(1)} %convert_element_type.93), channel_id=1, source_target_pairs={{24,0},{28,4},{25,1},{29,5},{26,2},{30,6},{27,3},{31,7}} | collective-permute-start | bytes 1179656 | tf_op jit(solution)/shard_map/ppermute | solution.py:23
  208.4 45.8 %collective-permute-start.10 = (bf16[2,512,768]{2,1,0:T(8,128)(2,1)S(1)}, bf16[2,512,768]{2,1,0:T(8,128)(2,1)S(1)}, u32[]{:S(2)}, u32[]{:S(2)}) collective-permute-start(bf16[2,512,768]{2,1,0:T(8,128)(2,1)S(1)} %fusion.10), channel_id=1, source_target_pairs={{0,4},{4,0},{8,12},{12,8},{16,20},{20,16},{24,28},{28,24},{1,5},{5... | collective-permute-start | bytes 4718600 | tf_op jit(solution)/shard_map/ppermute | solution.py:28
  221.0 10.7 %collective-permute-start.13 = (bf16[2,128,768]{2,1,0:T(8,128)(2,1)S(1)}, bf16[2,128,768]{2,1,0:T(8,128)(2,1)S(1)}, u32[]{:S(2)}, u32[]{:S(2)}) collective-permute-start(bf16[2,128,768]{2,1,0:T(8,128)(2,1)S(1)} %fusion.9), channel_id=1, source_target_pairs={{12,0},{16,4},{20,8},{24,12},{28,16},{13,1},{17,5},{21,9},{25,13},... | collective-permute-start | bytes 1179656 | tf_op jit(solution)/shard_map/ppermute | solution.py:23
  232.0 23.9 %copy-start = (bf16[2,512,768]{2,1,0:T(8,128)(2,1)}, bf16[2,512,768]{2,1,0:T(8,128)(2,1)S(1)}, u32[]{:S(2)}) copy-start(bf16[2,512,768]{2,1,0:T(8,128)(2,1)S(1)} %get-tuple-element.33) | copy-start | bytes 4718596
  234.1 49.8 %collective-permute-start.14 = (bf16[2,512,768]{2,1,0:T(8,128)(2,1)}, bf16[2,512,768]{2,1,0:T(8,128)(2,1)}, u32[]{:S(2)}, u32[]{:S(2)}) collective-permute-start(bf16[2,512,768]{2,1,0:T(8,128)(2,1)} %fusion.12), channel_id=1, source_target_pairs={{0,4},{4,0},{8,12},{12,8},{16,20},{20,16},{24,28},{28,24},{1,5},{5... | collective-permute-start | bytes 4718600 | tf_op jit(solution)/shard_map/ppermute | solution.py:28
  254.2 1.7 copy-start.12
  255.9 38.1 %collective-permute-start.11 = (bf16[2,512,768]{2,1,0:T(8,128)(2,1)}, bf16[2,512,768]{2,1,0:T(8,128)(2,1)}, u32[]{:S(2)}, u32[]{:S(2)}) collective-permute-start(bf16[2,512,768]{2,1,0:T(8,128)(2,1)} %fusion.6), channel_id=1, source_target_pairs={{8,0},{12,4},{16,8},{20,12},{24,16},{28,20},{9,1},{13,5},{17,9},{2... | collective-permute-start | bytes 4718600 | tf_op jit(solution)/shard_map/ppermute | solution.py:23
  257.2 26.7 %copy-start.1 = (bf16[2,512,768]{2,1,0:T(8,128)(2,1)S(1)}, bf16[2,512,768]{2,1,0:T(8,128)(2,1)}, u32[]{:S(2)}) copy-start(bf16[2,512,768]{2,1,0:T(8,128)(2,1)} %copy-done) | copy-start | bytes 4718596
  257.2 31.0 %all-to-all-start = ((bf16[4,128,768]{2,1,0:T(8,128)(2,1)}), bf16[4,128,768]{2,1,0:T(8,128)(2,1)}, u32[]{:S(2)}, u32[]{:S(2)}) async-start(bf16[4,128,768]{2,1,0:T(8,128)(2,1)} %bitcast.8), calls=%async_computation | async-start | bytes 1572864 | tf_op jit(solution)/shard_map/all_to_all | solution.py:228
  286.9 34.5 %collective-permute-start.15 = (bf16[2,512,768]{2,1,0:T(8,128)(2,1)}, bf16[2,512,768]{2,1,0:T(8,128)(2,1)}, u32[]{:S(2)}, u32[]{:S(2)}) collective-permute-start(bf16[2,512,768]{2,1,0:T(8,128)(2,1)} %fusion.7), channel_id=1, source_target_pairs={{8,0},{12,4},{16,8},{20,12},{24,16},{28,20},{9,1},{13,5},{17,9},{2... | collective-permute-start | bytes 4718600 | tf_op jit(solution)/shard_map/ppermute | solution.py:23
  288.2 15.1 %all-to-all-start.1 = ((bf16[4,128,768]{2,1,0:T(8,128)(2,1)}), bf16[4,128,768]{2,1,0:T(8,128)(2,1)S(1)}, u32[]{:S(2)}, u32[]{:S(2)}) async-start(bf16[4,128,768]{2,1,0:T(8,128)(2,1)} %bitcast.16), calls=%async_computation.1 | async-start | bytes 1572864 | tf_op jit(solution)/shard_map/all_to_all | solution.py:228
  291.7 2.3 copy-start.13
  304.2 23.6 %all-to-all-start.2 = ((bf16[2,512,768]{2,0,1:T(2,128)(2,1)}), bf16[2,512,768]{2,0,1:T(2,128)(2,1)S(1)}, u32[]{:S(2)}, u32[]{:S(2)}) async-start(bf16[2,512,768]{2,0,1:T(2,128)(2,1)} %copy.31), calls=%async_computation.2 | async-start | bytes 3145728 | tf_op jit(solution)/shard_map/all_to_all | solution.py:215
  327.8 23.6 %all-to-all-start.3 = ((bf16[2,512,768]{2,0,1:T(2,128)(2,1)}), bf16[2,512,768]{2,0,1:T(2,128)(2,1)S(1)}, u32[]{:S(2)}, u32[]{:S(2)}) async-start(bf16[2,512,768]{2,0,1:T(2,128)(2,1)} %copy.33), calls=%async_computation.3 | async-start | bytes 3145728 | tf_op jit(solution)/shard_map/all_to_all | solution.py:215
  (4 other events, 4.3 us)

commit v4 on v2

--- a/solution.py
+++ b/solution.py
@@ -160,7 +160,7 @@
     info = jnp.concatenate([me.astype(jnp.int32)[None], groups])
     odd = me % 2 == 1
     jumps = []
-    reached = REACH + 1
+    reached = 2 * REACH
     while reached < n_ctx:
         jumps.append(reached)
         reached *= 2
@@ -175,17 +175,17 @@
 
     def gathered(kv0, kv2, here):
         kv1 = swapped(jnp.where(here % 2 == 1, kv2, kv0), "ctx")
+        away = here - owner
         tiles = []
         for s in range(n_sum):
             at = (0, local_start[s], 0)
             size = (2, BLOCK, part)
             far = lax.dynamic_slice(kv2, at, size)
-            near = lax.dynamic_slice(kv1, at, size)
             own = lax.dynamic_slice(kv0, at, size)
-            tiles.append(
-                jnp.where(distance[s] == 2, far, jnp.where(distance[s] == 1, near, own))
-            )
+            tiles.append(jnp.where(away[s] == 2, far, own))
         kvs = jnp.concatenate(tiles, axis=1)
+        got = shifted(kvs, "ctx", 1)
+        kvs = jnp.where((tile_distance == 1) | (tile_distance == 3), got, kvs)
         for jump in jumps:
             got = shifted(kvs, "ctx", jump)
             kvs = jnp.where((tile_distance >= jump) & (tile_distance < 2 * jump), got, kvs)
@@ -195,6 +195,8 @@
         for jump in reversed(jumps):
             got = shifted(ps.astype(jnp.bfloat16), "ctx", -jump).astype(jnp.float32)
             ps = jnp.where((tile_distance >= 0) & (tile_distance < jump), ps + got, ps)
+        got = shifted(ps.astype(jnp.bfloat16), "ctx", -1).astype(jnp.float32)
+        ps = jnp.where((tile_distance == 0) | (tile_distance == 2), ps + got, ps)
 
         def add_tile(array, s, away):
             at = (0, local_start[s], 0)
@@ -204,7 +206,6 @@
 
         for s in range(n_sum):
             p2 = add_tile(p2, s, 2)
-            p1 = add_tile(p1, s, 1)
             p0 = add_tile(p0, s, 0)
         near = swapped(p1, "ctx")
         wide = near.astype(jnp.float32)

time: 333 us -> 361 us (1.084)
  starting transfers between devices: 101 us -> 119 us
  local copies, waits for them, and re-layouts: 31.6 us -> 37.7 us
    ppermute x18, starting transfers between devices: 63.7 us -> 83.5 us  [shifted(): lax.ppermute(value, axis, [(source, source + steps) for source in range(l...]
    ppermute x18, waiting for transfers between devices: 80.7 us -> 96.1 us  [shifted(): lax.ppermute(value, axis, [(source, source + steps) for source in range(l...]
    all_to_all x3, waiting for transfers between devices: 7.92 us -> 0.01 us  [on_device(): moved_q = lax.all_to_all(gq, 'tp', split_axis=0, concat_axis=1, tiled=True)]
    ppermute x6, waiting for transfers between devices: 9.27 us -> 1.93 us  [swapped(): lax.ppermute(value, axis, [(source, source ^ 1) for source in range(count)])]
    unnamed x84 -> x90, local copies, waits for them, and re-layouts: 13.6 us -> 20.3 us
    dynamic_update_slice x9 -> x6, other arithmetic: 8.27 us -> 7.76 us  [add_tile(): lax.dynamic_update_slice(array, (piece + term).astype(array.dtype), at)]
  transfers between devices with their start and end apart: 30 -> 30, of which waited for: 17 -> 13; matrix products, arithmetic and copies ran while one was open for 15% -> 13% of each run, Pallas kernels for 14% -> 14%
where the time goes in v4:
time: 361 us; the launch traced here: 356 us
  starting transfers between devices  119 us (33%)
  waiting for transfers between devices  107 us (30%)
  Pallas kernels  48.3 us (13%)
  other arithmetic  39 us (11%)
  local copies, waits for them, and re-layouts  37.7 us (10%)
  between operations  4.62 us (1%)
    ppermute x18, waiting for transfers between devices, shifted(): lax.ppermute(value, axis, [(source, source + steps) for source in range(l...  96.1 us
    ppermute x18, starting transfers between devices, shifted(): lax.ppermute(value, axis, [(source, source + steps) for source in range(l...  83.5 us
    pallas_call x3, Pallas kernels, attention(): pl.pallas_call(functools.partial(attend, n_sum), grid=(heads,), in_specs=...  48.3 us
    unnamed x90, local copies, waits for them, and re-layouts  20.3 us
    all_to_all x3, starting transfers between devices, on_device(): moved_q = lax.all_to_all(gq, 'tp', split_axis=0, concat_axis=1, tiled=True)  12.4 us
    ppermute x6, starting transfers between devices, swapped(): lax.ppermute(value, axis, [(source, source ^ 1) for source in range(count)])  11.7 us
    all_to_all x3, starting transfers between devices, returned(): lax.all_to_all(total, 'tp', split_axis=1, concat_axis=2, tiled=True)  11.5 us
    all_to_all x3, waiting for transfers between devices, returned(): lax.all_to_all(total, 'tp', split_axis=1, concat_axis=2, tiled=True)  9.21 us
  transfers between devices with their start and end apart: 30, of which 13 were waited for; matrix products, arithmetic and copies ran while one was open for 13% of the time, Pallas kernels for 14%

profile of v4, /device:TPU:0, one launch (start us, length us, event | category | flops | bytes accessed | tf_op | source)
XLA Modules:
  0.0 356.1 jit_solution(11846299964470860862)
XLA Ops:
  3.9 5.0 %collective-permute-start = (bf16[2,512,512]{2,1,0:T(8,128)(2,1)}, bf16[2,512,512]{2,1,0:T(8,128)(2,1)S(1)}, u32[]{:S(2)}, u32[]{:S(2)}) collective-permute-start(bf16[2,512,512]{2,1,0:T(8,128)(2,1)} %pad_maximum_fusion.2.kv0), channel_id=1, source_target_pairs={{0,8},{4,12},{8,16},{12,20},{16,24},{20,28},{1,9},{5,13},{9,17},{1... | collective-permute-start | bytes 3145736 | tf_op jit(solution)/shard_map/ppermute | solution.py:23
  10.0 3.5 collective-permute-start.4
  14.6 3.5 collective-permute-start.8
  18.8 13.9 %collective-permute-done.kv2 = bf16[2,512,512]{2,1,0:T(8,128)(2,1)S(1)} collective-permute-done((bf16[2,512,512]{2,1,0:T(8,128)(2,1)}, bf16[2,512,512]{2,1,0:T(8,128)(2,1)S(1)}, u32[]{:S(2)}, u32[]{:S(2)}) %collective-permute-start) | collective-permute-done | bytes 1048608 | tf_op jit(solution)/shard_map/ppermute | solution.py:23
  34.2 3.4 collective-permute-start.2
  42.2 12.9 %collective-permute-done.4.kv2 = bf16[2,512,512]{2,1,0:T(8,128)(2,1)S(1)} collective-permute-done((bf16[2,512,512]{2,1,0:T(8,128)(2,1)}, bf16[2,512,512]{2,1,0:T(8,128)(2,1)S(1)}, u32[]{:S(2)}, u32[]{:S(2)}) %collective-permute-start.4) | collective-permute-done | bytes 1048608 | tf_op jit(solution)/shard_map/ppermute | solution.py:23
  55.3 3.4 collective-permute-start.6
  62.3 27.4 %collective-permute-start.3 = (bf16[2,128,512]{2,1,0:T(8,128)(2,1)S(1)}, bf16[2,128,512]{2,1,0:T(8,128)(2,1)S(1)}, u32[]{:S(2)}, u32[]{:S(2)}) collective-permute-start(bf16[2,128,512]{2,1,0:T(8,128)(2,1)S(1)} %broadcast_select_fusion.5), channel_id=1, source_target_pairs={{0,16},{4,20},{8,24},{12,28},{1,17},{5,21},{9,25},{13,29},{2,18},{... | collective-permute-start | bytes 786440 | tf_op jit(solution)/shard_map/ppermute | solution.py:23
  89.9 16.6 %collective-permute-start.7 = (bf16[2,128,512]{2,1,0:T(8,128)(2,1)S(1)}, bf16[2,128,512]{2,1,0:T(8,128)(2,1)S(1)}, u32[]{:S(2)}, u32[]{:S(2)}) collective-permute-start(bf16[2,128,512]{2,1,0:T(8,128)(2,1)S(1)} %broadcast_select_fusion.4), channel_id=1, source_target_pairs={{0,16},{4,20},{8,24},{12,28},{1,17},{5,21},{9,25},{13,29},{2,18},{... | collective-permute-start | bytes 786440 | tf_op jit(solution)/shard_map/ppermute | solution.py:23
  106.7 3.7 %collective-permute-done.7 = bf16[2,128,512]{2,1,0:T(8,128)(2,1)S(1)} collective-permute-done((bf16[2,128,512]{2,1,0:T(8,128)(2,1)S(1)}, bf16[2,128,512]{2,1,0:T(8,128)(2,1)S(1)}, u32[]{:S(2)}, u32[]{:S(2)}) %collective-permute-start.7) | collective-permute-done | bytes 262176 | tf_op jit(solution)/shard_map/ppermute | solution.py:23
  114.5 16.1 %shard_map.76 = (bf16[512,512]{1,0:T(8,128)(2,1)S(1)}, bf16[2,512,512]{2,1,0:T(8,128)(2,1)S(1)}, bf16[2,512,512]{2,1,0:T(8,128)(2,1)S(1)}, f32[2,512,512]{2,1,0:...) custom-call(s32[2]{0:T(128)S(1)} %pad_add_fusion.info, bf16[512,1536]{1,0:T(8,128)(2,1)S(1)} %copy-done.17, ...), custom_call_target="tpu_custom_call" | custom-call | flops 3355443200 | bytes 8388608 | tf_op jit(solution)/shard_map/pallas_call | solution.py:111
  143.4 16.2 %shard_map.77 = (bf16[512,512]{1,0:T(8,128)(2,1)S(1)}, bf16[2,512,512]{2,1,0:T(8,128)(2,1)S(1)}, bf16[2,512,512]{2,1,0:T(8,128)(2,1)}, f32[2,512,512]{2,1,0:T(8,...) custom-call(s32[2]{0:T(128)S(1)} %pad_add_fusion.info, bf16[512,1536]{1,0:T(8,128)(2,1)S(1)} %copy-done.18, ...), custom_call_target="tpu_custom_call" | custom-call | flops 3355443200 | bytes 8388608 | tf_op jit(solution)/shard_map/pallas_call | solution.py:111
  167.0 2.7 collective-permute-start.10
  169.7 4.1 %all-to-all-start.1 = ((bf16[4,128,512]{2,1,0:T(8,128)(2,1)}), bf16[4,128,512]{2,1,0:T(8,128)(2,1)}, u32[]{:S(2)}, u32[]{:S(2)}) async-start(bf16[4,128,512]{2,1,0:T(8,128)(2,1)} %bitcast.54), calls=%async_computation.1 | async-start | bytes 1048576 | tf_op jit(solution)/shard_map/all_to_all | solution.py:228
  175.3 10.3 %collective-permute-done.10 = bf16[2,128,512]{2,1,0:T(8,128)(2,1)} collective-permute-done((bf16[2,128,512]{2,1,0:T(8,128)(2,1)}, bf16[2,128,512]{2,1,0:T(8,128)(2,1)}, u32[]{:S(2)}, u32[]{:S(2)}) %collective-permute-start.10) | collective-permute-done | bytes 262176 | tf_op jit(solution)/shard_map/ppermute | solution.py:23
  188.2 6.1 %collective-permute-start.11 = (bf16[2,128,512]{2,1,0:T(8,128)(2,1)S(1)}, bf16[2,128,512]{2,1,0:T(8,128)(2,1)S(1)}, u32[]{:S(2)}, u32[]{:S(2)}) collective-permute-start(bf16[2,128,512]{2,1,0:T(8,128)(2,1)S(1)} %broadcast_select_fusion.3), channel_id=1, source_target_pairs={{0,16},{4,20},{8,24},{12,28},{1,17},{5,21},{9,25},{13,29},{2,18},{... | collective-permute-start | bytes 786440 | tf_op jit(solution)/shard_map/ppermute | solution.py:23
  199.6 10.4 %collective-permute-done.14 = bf16[2,128,512]{2,1,0:T(8,128)(2,1)S(1)} collective-permute-done((bf16[2,128,512]{2,1,0:T(8,128)(2,1)S(1)}, bf16[2,128,512]{2,1,0:T(8,128)(2,1)S(1)}, u32[]{:S(2)}, u32[]{:S(2)}) %collective-permute-start.14) | collective-permute-done | bytes 262176 | tf_op jit(solution)/shard_map/ppermute | solution.py:23
  215.2 16.1 %shard_map.78 = (bf16[512,512]{1,0:T(8,128)(2,1)S(1)}, bf16[2,512,512]{2,1,0:T(8,128)(2,1)S(1)}, bf16[2,512,512]{2,1,0:T(8,128)(2,1)}, f32[2,512,512]{2,1,0:T(8,...) custom-call(s32[2]{0:T(128)S(1)} %pad_add_fusion.info, bf16[512,1536]{1,0:T(8,128)(2,1)S(1)} %copy-done.19, ...), custom_call_target="tpu_custom_call" | custom-call | flops 3355443200 | bytes 8388608 | tf_op jit(solution)/shard_map/pallas_call | solution.py:111
  239.2 4.1 %all-to-all-start = ((bf16[4,128,512]{2,1,0:T(8,128)(2,1)}), bf16[4,128,512]{2,1,0:T(8,128)(2,1)}, u32[]{:S(2)}, u32[]{:S(2)}) async-start(bf16[4,128,512]{2,1,0:T(8,128)(2,1)} %bitcast.53), calls=%async_computation | async-start | bytes 1048576 | tf_op jit(solution)/shard_map/all_to_all | solution.py:228
  243.4 2.6 collective-permute-done.20
  252.8 4.2 %all-to-all-start.2 = ((bf16[4,128,512]{2,1,0:T(8,128)(2,1)}), bf16[4,128,512]{2,1,0:T(8,128)(2,1)}, u32[]{:S(2)}, u32[]{:S(2)}) async-start(bf16[4,128,512]{2,1,0:T(8,128)(2,1)} %bitcast.55), calls=%async_computation.2 | async-start | bytes 1048576 | tf_op jit(solution)/shard_map/all_to_all | solution.py:228
  257.0 5.4 %collective-permute-done.21 = bf16[2,128,512]{2,1,0:T(8,128)(2,1)} collective-permute-done((bf16[2,128,512]{2,1,0:T(8,128)(2,1)}, bf16[2,128,512]{2,1,0:T(8,128)(2,1)}, u32[]{:S(2)}, u32[]{:S(2)}) %collective-permute-start.21) | collective-permute-done | bytes 262176 | tf_op jit(solution)/shard_map/ppermute | solution.py:23
  264.4 11.3 %collective-permute-done.15 = bf16[2,512,512]{2,1,0:T(8,128)(2,1)} collective-permute-done((bf16[2,512,512]{2,1,0:T(8,128)(2,1)}, bf16[2,512,512]{2,1,0:T(8,128)(2,1)}, u32[]{:S(2)}, u32[]{:S(2)}) %collective-permute-start.15) | collective-permute-done | bytes 1048608 | tf_op jit(solution)/shard_map/ppermute | solution.py:23
  280.1 3.5 all-to-all-start.3
  283.7 2.7 fusion.11
  287.9 13.4 %collective-permute-done.19 = bf16[2,512,512]{2,1,0:T(8,128)(2,1)} collective-permute-done((bf16[2,512,512]{2,1,0:T(8,128)(2,1)}, bf16[2,512,512]{2,1,0:T(8,128)(2,1)}, u32[]{:S(2)}, u32[]{:S(2)}) %collective-permute-start.19) | collective-permute-done | bytes 1048608 | tf_op jit(solution)/shard_map/ppermute | solution.py:23
  305.3 3.5 all-to-all-start.4
  311.0 10.6 %collective-permute-done.23 = bf16[2,512,512]{2,1,0:T(8,128)(2,1)} collective-permute-done((bf16[2,512,512]{2,1,0:T(8,128)(2,1)}, bf16[2,512,512]{2,1,0:T(8,128)(2,1)}, u32[]{:S(2)}, u32[]{:S(2)}) %collective-permute-start.23) | collective-permute-done | bytes 1048608 | tf_op jit(solution)/shard_map/ppermute | solution.py:23
  321.6 2.7 fusion.8
  326.3 4.5 %all-to-all-start.5 = ((bf16[2,512,512]{2,0,1:T(2,128)(2,1)}), bf16[2,512,512]{2,0,1:T(2,128)(2,1)}, u32[]{:S(2)}, u32[]{:S(2)}) async-start(bf16[2,512,512]{2,0,1:T(2,128)(2,1)} %copy.40), calls=%async_computation.5 | async-start | bytes 2097152 | tf_op jit(solution)/shard_map/all_to_all | solution.py:215
  335.9 9.2 %all-to-all-done.5 = bf16[2,512,512]{2,0,1:T(2,128)(2,1)} async-done(((bf16[2,512,512]{2,0,1:T(2,128)(2,1)}), bf16[2,512,512]{2,0,1:T(2,128)(2,1)}, u32[]{:S(2)}, u32[]{:S(2)}) %all-to-all-start.5) | async-done | bytes 1048608 | tf_op jit(solution)/shard_map/all_to_all | solution.py:215
  349.2 2.7 copy.45
  (171 shorter events, 95.7 us)
Async XLA Ops:
  3.9 28.8 %collective-permute-start = (bf16[2,512,512]{2,1,0:T(8,128)(2,1)}, bf16[2,512,512]{2,1,0:T(8,128)(2,1)S(1)}, u32[]{:S(2)}, u32[]{:S(2)}) collective-permute-start(bf16[2,512,512]{2,1,0:T(8,128)(2,1)} %pad_maximum_fusion.2.kv0), channel_id=1, source_target_pairs={{0,8},{4,12},{8,16},{12,20},{16,24},{20,28},{1,9},{5,13},{9,17},{1... | collective-permute-start | bytes 3145736 | tf_op jit(solution)/shard_map/ppermute | solution.py:23
  10.0 45.2 %collective-permute-start.4 = (bf16[2,512,512]{2,1,0:T(8,128)(2,1)}, bf16[2,512,512]{2,1,0:T(8,128)(2,1)S(1)}, u32[]{:S(2)}, u32[]{:S(2)}) collective-permute-start(bf16[2,512,512]{2,1,0:T(8,128)(2,1)} %pad_maximum_fusion.3.kv0), channel_id=1, source_target_pairs={{0,8},{4,12},{8,16},{12,20},{16,24},{20,28},{1,9},{5,13},{9,17},{1... | collective-permute-start | bytes 3145736 | tf_op jit(solution)/shard_map/ppermute | solution.py:23
  14.6 151.6 %collective-permute-start.8 = (bf16[2,512,512]{2,1,0:T(8,128)(2,1)}, bf16[2,512,512]{2,1,0:T(8,128)(2,1)S(1)}, u32[]{:S(2)}, u32[]{:S(2)}) collective-permute-start(bf16[2,512,512]{2,1,0:T(8,128)(2,1)} %pad_maximum_fusion.4.kv0), channel_id=1, source_target_pairs={{0,8},{4,12},{8,16},{12,20},{16,24},{20,28},{1,9},{5,13},{9,17},{1... | collective-permute-start | bytes 3145736 | tf_op jit(solution)/shard_map/ppermute | solution.py:23
  34.2 28.1 %collective-permute-start.2 = (bf16[2,128,512]{2,1,0:T(8,128)(2,1)S(1)}, bf16[2,128,512]{2,1,0:T(8,128)(2,1)S(1)}, u32[]{:S(2)}, u32[]{:S(2)}) collective-permute-start(bf16[2,128,512]{2,1,0:T(8,128)(2,1)S(1)} %fusion.23), channel_id=1, source_target_pairs={{0,4},{4,8},{8,12},{12,16},{16,20},{20,24},{24,28},{1,5},{5,9},{9,... | collective-permute-start | bytes 786440 | tf_op jit(solution)/shard_map/ppermute | solution.py:23
  39.9 70.5 %collective-permute-start.1 = (bf16[2,512,512]{2,1,0:T(8,128)(2,1)}, bf16[2,512,512]{2,1,0:T(8,128)(2,1)}, u32[]{:S(2)}, u32[]{:S(2)}) collective-permute-start(bf16[2,512,512]{2,1,0:T(8,128)(2,1)} %broadcast_select_fusion.2), channel_id=1, source_target_pairs={{0,4},{4,0},{8,12},{12,8},{16,20},{20,16},{24,28},{28,24},{1,5},{5... | collective-permute-start | bytes 3145736 | tf_op jit(solution)/shard_map/ppermute | solution.py:28
  55.2 34.6 %copy-start.4 = (bf16[2,512,512]{2,1,0:T(8,128)(2,1)}, bf16[2,512,512]{2,1,0:T(8,128)(2,1)S(1)}, u32[]{:S(2)}) copy-start(bf16[2,512,512]{2,1,0:T(8,128)(2,1)S(1)} %collective-permute-done.4.kv2) | copy-start | bytes 3145732
  55.3 34.5 %collective-permute-start.6 = (bf16[2,128,512]{2,1,0:T(8,128)(2,1)S(1)}, bf16[2,128,512]{2,1,0:T(8,128)(2,1)S(1)}, u32[]{:S(2)}, u32[]{:S(2)}) collective-permute-start(bf16[2,128,512]{2,1,0:T(8,128)(2,1)S(1)} %fusion.21), channel_id=1, source_target_pairs={{0,4},{4,8},{8,12},{12,16},{16,20},{20,24},{24,28},{1,5},{5,9},{9,... | collective-permute-start | bytes 786440 | tf_op jit(solution)/shard_map/ppermute | solution.py:23
  59.9 79.5 %collective-permute-start.5 = (bf16[2,512,512]{2,1,0:T(8,128)(2,1)}, bf16[2,512,512]{2,1,0:T(8,128)(2,1)}, u32[]{:S(2)}, u32[]{:S(2)}) collective-permute-start(bf16[2,512,512]{2,1,0:T(8,128)(2,1)} %broadcast_select_fusion.1), channel_id=1, source_target_pairs={{0,4},{4,0},{8,12},{12,8},{16,20},{20,16},{24,28},{28,24},{1,5},{5... | collective-permute-start | bytes 3145736 | tf_op jit(solution)/shard_map/ppermute | solution.py:28
  62.3 44.3 %collective-permute-start.3 = (bf16[2,128,512]{2,1,0:T(8,128)(2,1)S(1)}, bf16[2,128,512]{2,1,0:T(8,128)(2,1)S(1)}, u32[]{:S(2)}, u32[]{:S(2)}) collective-permute-start(bf16[2,128,512]{2,1,0:T(8,128)(2,1)S(1)} %broadcast_select_fusion.5), channel_id=1, source_target_pairs={{0,16},{4,20},{8,24},{12,28},{1,17},{5,21},{9,25},{13,29},{2,18},{... | collective-permute-start | bytes 786440 | tf_op jit(solution)/shard_map/ppermute | solution.py:23
  89.9 20.5 %collective-permute-start.7 = (bf16[2,128,512]{2,1,0:T(8,128)(2,1)S(1)}, bf16[2,128,512]{2,1,0:T(8,128)(2,1)S(1)}, u32[]{:S(2)}, u32[]{:S(2)}) collective-permute-start(bf16[2,128,512]{2,1,0:T(8,128)(2,1)S(1)} %broadcast_select_fusion.4), channel_id=1, source_target_pairs={{0,16},{4,20},{8,24},{12,28},{1,17},{5,21},{9,25},{13,29},{2,18},{... | collective-permute-start | bytes 786440 | tf_op jit(solution)/shard_map/ppermute | solution.py:23
  138.0 50.1 %collective-permute-start.13 = (bf16[2,128,512]{2,1,0:T(8,128)(2,1)}, bf16[2,128,512]{2,1,0:T(8,128)(2,1)}, u32[]{:S(2)}, u32[]{:S(2)}) collective-permute-start(bf16[2,128,512]{2,1,0:T(8,128)(2,1)} %convert_element_type.102), channel_id=1, source_target_pairs={{16,0},{20,4},{24,8},{28,12},{17,1},{21,5},{25,9},{29,13},{18,2},{... | collective-permute-start | bytes 786440 | tf_op jit(solution)/shard_map/ppermute | solution.py:23
  139.3 74.0 %collective-permute-start.12 = (bf16[2,512,512]{2,1,0:T(8,128)(2,1)}, bf16[2,512,512]{2,1,0:T(8,128)(2,1)S(1)}, u32[]{:S(2)}, u32[]{:S(2)}) collective-permute-start(bf16[2,512,512]{2,1,0:T(8,128)(2,1)} %copy-done.23), channel_id=1, source_target_pairs={{0,4},{4,0},{8,12},{12,8},{16,20},{20,16},{24,28},{28,24},{1,5},{5... | collective-permute-start | bytes 3145736 | tf_op jit(solution)/shard_map/ppermute | solution.py:28
  162.8 32.5 %collective-permute-start.16 = (bf16[2,128,512]{2,1,0:T(8,128)(2,1)}, bf16[2,128,512]{2,1,0:T(8,128)(2,1)S(1)}, u32[]{:S(2)}, u32[]{:S(2)}) collective-permute-start(bf16[2,128,512]{2,1,0:T(8,128)(2,1)} %convert_element_type.113), channel_id=1, source_target_pairs={{16,0},{20,4},{24,8},{28,12},{17,1},{21,5},{25,9},{29,13},{18,2},{... | collective-permute-start | bytes 786440 | tf_op jit(solution)/shard_map/ppermute | solution.py:23
  164.1 84.9 %collective-permute-start.18 = (bf16[2,512,512]{2,1,0:T(8,128)(2,1)}, bf16[2,512,512]{2,1,0:T(8,128)(2,1)}, u32[]{:S(2)}, u32[]{:S(2)}) collective-permute-start(bf16[2,512,512]{2,1,0:T(8,128)(2,1)} %get-tuple-element.29), channel_id=1, source_target_pairs={{0,4},{4,0},{8,12},{12,8},{16,20},{20,16},{24,28},{28,24},{1,5},{5... | collective-permute-start | bytes 3145736 | tf_op jit(solution)/shard_map/ppermute | solution.py:28
  167.0 18.6 %collective-permute-start.10 = (bf16[2,128,512]{2,1,0:T(8,128)(2,1)}, bf16[2,128,512]{2,1,0:T(8,128)(2,1)}, u32[]{:S(2)}, u32[]{:S(2)}) collective-permute-start(bf16[2,128,512]{2,1,0:T(8,128)(2,1)} %fusion.19), channel_id=1, source_target_pairs={{0,4},{4,8},{8,12},{12,16},{16,20},{20,24},{24,28},{1,5},{5,9},{9,... | collective-permute-start | bytes 786440 | tf_op jit(solution)/shard_map/ppermute | solution.py:23
  169.7 69.6 %all-to-all-start.1 = ((bf16[4,128,512]{2,1,0:T(8,128)(2,1)}), bf16[4,128,512]{2,1,0:T(8,128)(2,1)}, u32[]{:S(2)}, u32[]{:S(2)}) async-start(bf16[4,128,512]{2,1,0:T(8,128)(2,1)} %bitcast.54), calls=%async_computation.1 | async-start | bytes 1048576 | tf_op jit(solution)/shard_map/all_to_all | solution.py:228
  175.3 34.8 %copy-start.9 = (bf16[2,512,512]{2,1,0:T(8,128)(2,1)S(1)}, bf16[2,512,512]{2,1,0:T(8,128)(2,1)}, u32[]{:S(2)}) copy-start(bf16[2,512,512]{2,1,0:T(8,128)(2,1)} %copy-done.8) | copy-start | bytes 3145732
  185.5 29.7 %collective-permute-start.9 = (bf16[2,512,512]{2,1,0:T(8,128)(2,1)S(1)}, bf16[2,512,512]{2,1,0:T(8,128)(2,1)S(1)}, u32[]{:S(2)}, u32[]{:S(2)}) collective-permute-start(bf16[2,512,512]{2,1,0:T(8,128)(2,1)S(1)} %broadcast_select_fusion), channel_id=1, source_target_pairs={{0,4},{4,0},{8,12},{12,8},{16,20},{20,16},{24,28},{28,24},{1,5},{5... | collective-permute-start | bytes 3145736 | tf_op jit(solution)/shard_map/ppermute | solution.py:28
  188.2 10.0 %collective-permute-start.11 = (bf16[2,128,512]{2,1,0:T(8,128)(2,1)S(1)}, bf16[2,128,512]{2,1,0:T(8,128)(2,1)S(1)}, u32[]{:S(2)}, u32[]{:S(2)}) collective-permute-start(bf16[2,128,512]{2,1,0:T(8,128)(2,1)S(1)} %broadcast_select_fusion.3), channel_id=1, source_target_pairs={{0,16},{4,20},{8,24},{12,28},{1,17},{5,21},{9,25},{13,29},{2,18},{... | collective-permute-start | bytes 786440 | tf_op jit(solution)/shard_map/ppermute | solution.py:23
  195.3 14.7 %collective-permute-start.14 = (bf16[2,128,512]{2,1,0:T(8,128)(2,1)S(1)}, bf16[2,128,512]{2,1,0:T(8,128)(2,1)S(1)}, u32[]{:S(2)}, u32[]{:S(2)}) collective-permute-start(bf16[2,128,512]{2,1,0:T(8,128)(2,1)S(1)} %fusion.12), channel_id=1, source_target_pairs={{4,0},{8,4},{12,8},{16,12},{20,16},{24,20},{28,24},{5,1},{9,5},{13... | collective-permute-start | bytes 786440 | tf_op jit(solution)/shard_map/ppermute | solution.py:23
  198.1 37.9 %collective-permute-start.17 = (bf16[2,128,512]{2,1,0:T(8,128)(2,1)S(1)}, bf16[2,128,512]{2,1,0:T(8,128)(2,1)S(1)}, u32[]{:S(2)}, u32[]{:S(2)}) collective-permute-start(bf16[2,128,512]{2,1,0:T(8,128)(2,1)S(1)} %fusion.13), channel_id=1, source_target_pairs={{4,0},{8,4},{12,8},{16,12},{20,16},{24,20},{28,24},{5,1},{9,5},{13... | collective-permute-start | bytes 786440 | tf_op jit(solution)/shard_map/ppermute | solution.py:23
  232.0 13.9 %collective-permute-start.20 = (bf16[2,128,512]{2,1,0:T(8,128)(2,1)}, bf16[2,128,512]{2,1,0:T(8,128)(2,1)}, u32[]{:S(2)}, u32[]{:S(2)}) collective-permute-start(bf16[2,128,512]{2,1,0:T(8,128)(2,1)} %convert_element_type.124), channel_id=1, source_target_pairs={{16,0},{20,4},{24,8},{28,12},{17,1},{21,5},{25,9},{29,13},{18,2},{... | collective-permute-start | bytes 786440 | tf_op jit(solution)/shard_map/ppermute | solution.py:23
  234.7 41.0 %collective-permute-start.15 = (bf16[2,512,512]{2,1,0:T(8,128)(2,1)}, bf16[2,512,512]{2,1,0:T(8,128)(2,1)}, u32[]{:S(2)}, u32[]{:S(2)}) collective-permute-start(bf16[2,512,512]{2,1,0:T(8,128)(2,1)} %fusion.9), channel_id=1, source_target_pairs={{8,0},{12,4},{16,8},{20,12},{24,16},{28,20},{9,1},{13,5},{17,9},{2... | collective-permute-start | bytes 3145736 | tf_op jit(solution)/shard_map/ppermute | solution.py:23
  236.7 46.9 %collective-permute-start.22 = (bf16[2,512,512]{2,1,0:T(8,128)(2,1)}, bf16[2,512,512]{2,1,0:T(8,128)(2,1)}, u32[]{:S(2)}, u32[]{:S(2)}) collective-permute-start(bf16[2,512,512]{2,1,0:T(8,128)(2,1)} %get-tuple-element.33), channel_id=1, source_target_pairs={{0,4},{4,0},{8,12},{12,8},{16,20},{20,16},{24,28},{28,24},{1,5},{5... | collective-permute-start | bytes 3145736 | tf_op jit(solution)/shard_map/ppermute | solution.py:28
  239.2 13.6 %all-to-all-start = ((bf16[4,128,512]{2,1,0:T(8,128)(2,1)}), bf16[4,128,512]{2,1,0:T(8,128)(2,1)}, u32[]{:S(2)}, u32[]{:S(2)}) async-start(bf16[4,128,512]{2,1,0:T(8,128)(2,1)} %bitcast.53), calls=%async_computation | async-start | bytes 1048576 | tf_op jit(solution)/shard_map/all_to_all | solution.py:228
  247.7 14.7 %collective-permute-start.21 = (bf16[2,128,512]{2,1,0:T(8,128)(2,1)}, bf16[2,128,512]{2,1,0:T(8,128)(2,1)}, u32[]{:S(2)}, u32[]{:S(2)}) collective-permute-start(bf16[2,128,512]{2,1,0:T(8,128)(2,1)} %fusion.14), channel_id=1, source_target_pairs={{4,0},{8,4},{12,8},{16,12},{20,16},{24,20},{28,24},{5,1},{9,5},{13... | collective-permute-start | bytes 786440 | tf_op jit(solution)/shard_map/ppermute | solution.py:23
  251.5 49.7 %collective-permute-start.19 = (bf16[2,512,512]{2,1,0:T(8,128)(2,1)}, bf16[2,512,512]{2,1,0:T(8,128)(2,1)}, u32[]{:S(2)}, u32[]{:S(2)}) collective-permute-start(bf16[2,512,512]{2,1,0:T(8,128)(2,1)} %fusion.10), channel_id=1, source_target_pairs={{8,0},{12,4},{16,8},{20,12},{24,16},{28,20},{9,1},{13,5},{17,9},{2... | collective-permute-start | bytes 3145736 | tf_op jit(solution)/shard_map/ppermute | solution.py:23
  252.8 27.3 %all-to-all-start.2 = ((bf16[4,128,512]{2,1,0:T(8,128)(2,1)}), bf16[4,128,512]{2,1,0:T(8,128)(2,1)}, u32[]{:S(2)}, u32[]{:S(2)}) async-start(bf16[4,128,512]{2,1,0:T(8,128)(2,1)} %bitcast.55), calls=%async_computation.2 | async-start | bytes 1048576 | tf_op jit(solution)/shard_map/all_to_all | solution.py:228
  280.1 25.2 %all-to-all-start.3 = ((bf16[2,512,512]{2,0,1:T(2,128)(2,1)}), bf16[2,512,512]{2,0,1:T(2,128)(2,1)S(1)}, u32[]{:S(2)}, u32[]{:S(2)}) async-start(bf16[2,512,512]{2,0,1:T(2,128)(2,1)} %copy.36), calls=%async_computation.3 | async-start | bytes 2097152 | tf_op jit(solution)/shard_map/all_to_all | solution.py:215
  286.3 35.3 %collective-permute-start.23 = (bf16[2,512,512]{2,1,0:T(8,128)(2,1)}, bf16[2,512,512]{2,1,0:T(8,128)(2,1)}, u32[]{:S(2)}, u32[]{:S(2)}) collective-permute-start(bf16[2,512,512]{2,1,0:T(8,128)(2,1)} %fusion.11), channel_id=1, source_target_pairs={{8,0},{12,4},{16,8},{20,12},{24,16},{28,20},{9,1},{13,5},{17,9},{2... | collective-permute-start | bytes 3145736 | tf_op jit(solution)/shard_map/ppermute | solution.py:23
  305.3 21.0 %all-to-all-start.4 = ((bf16[2,512,512]{2,0,1:T(2,128)(2,1)}), bf16[2,512,512]{2,0,1:T(2,128)(2,1)S(1)}, u32[]{:S(2)}, u32[]{:S(2)}) async-start(bf16[2,512,512]{2,0,1:T(2,128)(2,1)} %copy.38), calls=%async_computation.4 | async-start | bytes 2097152 | tf_op jit(solution)/shard_map/all_to_all | solution.py:215
  326.3 18.8 %all-to-all-start.5 = ((bf16[2,512,512]{2,0,1:T(2,128)(2,1)}), bf16[2,512,512]{2,0,1:T(2,128)(2,1)}, u32[]{:S(2)}, u32[]{:S(2)}) async-start(bf16[2,512,512]{2,0,1:T(2,128)(2,1)} %copy.40), calls=%async_computation.5 | async-start | bytes 2097152 | tf_op jit(solution)/shard_map/all_to_all | solution.py:215
  (42 other events, 343.5 us)
